TPU v7x, 512 devices: a whole 4x4x16 slice. The times are simulated.
512 devices in a mesh: gx: 32 (over z, core), gy: 16 (over x, y).
Axes of the slice: x: 4, y: 4, z: 16, core: 2. Of those that a mesh axis runs over, the one named last changes fastest.
Arguments:
- right_side: float32 [512, 256, 128], P('gx', 'gy'), may hold values from -96 to 96
- alpha_cells: float32 [512, 256, 128], P('gx', 'gy'), may hold values from 0.05 to 0.5
- beta_x: float32 [512, 256, 128], P('gx', 'gy'), may hold values from 0.5 to 2
- beta_y: float32 [512, 256, 128], P('gx', 'gy'), may hold values from 0.5 to 2
- beta_z: float32 [512, 256, 128], P('gx', 'gy'), may hold values from 0.5 to 2
Outputs:
- smooth_fine: float32 [512, 256, 128], P('gx', 'gy')
- smooth_one: float32 [256, 128, 64], P('gx', 'gy')
- bottom: float32 [128, 64, 32], P('gx', 'gy')
All inputs are finite; a program needn't handle non-finite values.
Results may differ from a plain program's by a relative error of at most 0.0003.
Values sent between devices are 32-bit elements; how exact they have to be, the bound alone decides.
A program may use at most 64 MiB of HBM per device.

v0:
```python
import jax
import jax.numpy as jnp
from jax import lax
from jax.sharding import PartitionSpec as P

BICG = 2


LMAX = 2.0
LMIN = 0.25


def passed_along(block, axis, distance):
    devices = range(lax.axis_size(axis))
    route = [(i - distance, i) for i in devices if i - distance in devices]
    return lax.ppermute(block, axis, route)


def extended(cells, sides, width):
    for axis, dim in sides:
        count = lax.axis_size(axis)
        ends = count - 1
        head = lax.slice_in_dim(cells, 0, width, axis=dim)
        tail = lax.slice_in_dim(cells, cells.shape[dim] - width, cells.shape[dim], axis=dim)
        cells = jnp.concatenate(
            [
                lax.ppermute(tail, axis, [(i, (i + 1) % count) for i in range(ends)]),
                cells,
                lax.ppermute(head, axis, [((i + 1) % count, i) for i in range(ends)]),
            ],
            axis=dim,
        )
    return cells


def next_face(coeff, axis):
    count = coeff.shape[axis]
    head = lax.slice_in_dim(coeff, 1, count, axis=axis)
    tail = jnp.zeros_like(lax.slice_in_dim(coeff, 0, 1, axis=axis))
    return jnp.concatenate([head, tail], axis)


def combine(padded, alpha, faces, scale):
    bx, by, bz, bxu, byu, bzu = faces
    field = padded[1:-1, 1:-1, 1:-1]
    flux = bxu * (padded[2:, 1:-1, 1:-1] - field) - bx * (field - padded[:-2, 1:-1, 1:-1])
    flux = flux + byu * (padded[1:-1, 2:, 1:-1] - field) - by * (field - padded[1:-1, :-2, 1:-1])
    flux = flux + bzu * (padded[1:-1, 1:-1, 2:] - field) - bz * (field - padded[1:-1, 1:-1, :-2])
    return alpha * field - scale * flux


def shared_faces(bx, by, bz):
    after_x = passed_along(bx[:1], "gx", -1)
    upper_x = jnp.concatenate([bx[1:], after_x], 0)
    after_y = passed_along(by[:, :1], "gy", -1)
    upper_y = jnp.concatenate([by[:, 1:], after_y], 1)
    return (bx, by, bz, upper_x, upper_y, next_face(bz, 2))


def spread_apply(alpha, faces, scale):

    def apply(field):
        edged = extended(field, (("gx", 0), ("gy", 1)), 1)
        padded = jnp.pad(edged, ((0, 0), (0, 0), (1, 1)))
        return combine(padded, alpha, faces, scale)

    return apply


def whole_apply(alpha, faces, scale):

    def apply(field):
        return combine(jnp.pad(field, 1), alpha, faces, scale)

    return apply


def chebyshev(rhs, alpha, faces, scale, apply):
    bx, by, bz, bxu, byu, bzu = faces
    inverse = 1.0 / (alpha + scale * (bx + bxu + by + byu + bz + bzu))
    theta = 0.5 * (LMAX + LMIN)
    delta = 0.5 * (LMAX - LMIN)
    sigma = theta / delta
    rho = 1.0 / sigma
    update = inverse * rhs / theta
    solved = update
    for sweep in range(3):
        resid = rhs - apply(solved)
        rho_next = 1.0 / (2.0 * sigma - rho)
        update = rho_next * rho * update + 2.0 * rho_next / delta * (inverse * resid)
        solved = solved + update
        rho = rho_next
    resid = rhs - apply(solved)
    return (solved, resid)


def restrict_cells(values):
    a, b, c = values.shape
    return values.reshape(a // 2, 2, b // 2, 2, c // 2, 2).mean(axis=(1, 3, 5))


def restrict_faces(bx, by, bz):
    a, b, c = bx.shape
    coarse_x = bx[0::2].reshape(a // 2, b // 2, 2, c // 2, 2).mean(axis=(2, 4))
    coarse_y = by[:, 0::2].reshape(a // 2, 2, b // 2, c // 2, 2).mean(axis=(1, 4))
    coarse_z = bz[:, :, 0::2].reshape(a // 2, 2, b // 2, 2, c // 2).mean(axis=(1, 3))
    return (coarse_x, coarse_y, coarse_z)


def whole_bicgstab(rhs, apply):
    solved = jnp.zeros_like(rhs)
    resid = rhs
    direction = rhs
    rho = jnp.sum(rhs * resid)
    for sweep in range(BICG):
        image = apply(direction)
        step = rho / jnp.sum(rhs * image)
        half = resid - step * image
        turned = apply(half)
        omega = jnp.sum(turned * half) / jnp.sum(turned * turned)
        solved = solved + step * direction + omega * half
        resid = half - omega * turned
        rho_next = jnp.sum(rhs * resid)
        factor = rho_next / rho * (step / omega)
        direction = resid + factor * (direction - omega * image)
        rho = rho_next
    return solved


def per_device(right_side, alpha_cells, beta_x, beta_y, beta_z):
    rhs, alpha, bx, by, bz = (right_side, alpha_cells, beta_x, beta_y, beta_z)
    scale = 16.0
    smoothed = []
    for level in range(2):
        faces = shared_faces(bx, by, bz)
        solved, resid = chebyshev(rhs, alpha, faces, scale, spread_apply(alpha, faces, scale))
        smoothed.append(solved)
        rhs = restrict_cells(resid)
        alpha = restrict_cells(alpha)
        bx, by, bz = restrict_faces(bx, by, bz)
        scale = scale * 0.25
    pieces = (
        lax.all_gather(rhs, "gx", axis=0, tiled=True),
        lax.all_gather(alpha, "gx", axis=0, tiled=True),
        lax.all_gather(bx, "gx", axis=0, tiled=True),
        lax.all_gather(by, "gx", axis=0, tiled=True),
        lax.all_gather(bz, "gx", axis=0, tiled=True),
    )
    whole = (
        lax.all_gather(pieces[0], "gy", axis=1, tiled=True),
        lax.all_gather(pieces[1], "gy", axis=1, tiled=True),
        lax.all_gather(pieces[2], "gy", axis=1, tiled=True),
        lax.all_gather(pieces[3], "gy", axis=1, tiled=True),
        lax.all_gather(pieces[4], "gy", axis=1, tiled=True),
    )
    rhs_whole, alpha_whole, bx_whole, by_whole, bz_whole = whole
    faces = (
        bx_whole,
        by_whole,
        bz_whole,
        next_face(bx_whole, 0),
        next_face(by_whole, 1),
        next_face(bz_whole, 2),
    )
    solved_whole = whole_bicgstab(rhs_whole, whole_apply(alpha_whole, faces, scale))
    rows = rhs.shape[0]
    columns = rhs.shape[1]
    first_row = lax.axis_index("gx") * rows
    first_col = lax.axis_index("gy") * columns
    bottom = lax.dynamic_slice(
        solved_whole, (first_row, first_col, jnp.int32(0)), (rows, columns, rhs.shape[2])
    )
    return (smoothed[0], smoothed[1], bottom)


def solution(mesh):
    placed = (
        P("gx", "gy", None),
        P("gx", "gy", None),
        P("gx", "gy", None),
        P("gx", "gy", None),
        P("gx", "gy", None),
    )
    return jax.shard_map(
        per_device,
        mesh=mesh,
        in_specs=placed,
        out_specs=(P("gx", "gy", None), P("gx", "gy", None), P("gx", "gy", None)),
        check_vma=False,
    )
```

profile of v0, /device:TPU:1, one launch (start us, length us, event | category | flops | bytes accessed | tf_op | source)
XLA Modules:
  0.0 451.8 jit_solution(9775150572609833515)
XLA Ops:
  10.0 38.3 %all_gather.34 = f32[128,4,32]{2,1,0:T(4,128)S(1)} all-gather(f32[4,4,32]{2,1,0:T(4,128)S(1)} %broadcast_multiply_fusion.8), channel_id=1, replica_groups=mesh['gx'=32,'gy'=16] {'gx'}, dimensions={0}, use_global_device_ids=true | all-gather | bytes 67584 | tf_op jit(solution)/shard_map/all_gather | solution.py:145
  49.1 2.1 collective-permute-start
  55.8 2.3 collective-permute-start.2
  58.2 4.1 collective-permute-start.3
  64.4 4.0 collective-permute-start.5
  68.4 30.5 %all_gather.36 = f32[128,4,32]{2,1,0:T(4,128)S(1)} all-gather(f32[4,4,32]{2,1,0:T(4,128)S(1)} %broadcast_multiply_fusion.7), channel_id=1, replica_groups=mesh['gx'=32,'gy'=16] {'gx'}, dimensions={0}, use_global_device_ids=true | all-gather | bytes 67584 | tf_op jit(solution)/shard_map/all_gather | solution.py:146
  100.3 2.1 collective-permute-start.6
  102.3 3.5 collective-permute-start.7
  107.9 4.0 collective-permute-start.9
  111.9 2.3 slice.518
  114.9 1.9 collective-permute-start.10
  116.9 4.8 %collective-permute-start.11 = (f32[1,16,128]{2,1,0:T(8,128)S(1)}, f32[1,16,128]{2,1,0:T(8,128)S(1)}, u32[]{:S(2)}, u32[]{:S(2)}) collective-permute-start(f32[1,16,128]{2,1,0:T(8,128)S(1)} %get-tuple-element.46), channel_id=1, source_target_pairs={{0,16},{16,32},{32,48},{48,64},{64,80},{80,96},{96,112},{112,128},... | collective-permute-start | bytes 24584 | tf_op jit(solution)/shard_map/ppermute | solution.py:27
  123.7 4.8 %collective-permute-start.13 = (f32[18,1,128]{2,1,0:T(1,128)S(1)}, f32[18,1,128]{2,1,0:T(1,128)S(1)}, u32[]{:S(2)}, u32[]{:S(2)}) collective-permute-start(f32[18,1,128]{2,1,0:T(1,128)S(1)} %get-tuple-element.38), channel_id=1, source_target_pairs={{0,1},{1,2},{2,3},{3,4},{4,5},{5,6},{6,7},{7,8},{8,9},{9,10},{10,1... | collective-permute-start | bytes 27656 | tf_op jit(solution)/shard_map/ppermute | solution.py:27
  130.0 1.9 collective-permute-start.16
  131.9 5.0 %collective-permute-start.17 = (f32[1,16,128]{2,1,0:T(8,128)S(1)}, f32[1,16,128]{2,1,0:T(8,128)S(1)}, u32[]{:S(2)}, u32[]{:S(2)}) collective-permute-start(f32[1,16,128]{2,1,0:T(8,128)S(1)} %get-tuple-element.44), channel_id=1, source_target_pairs={{0,16},{16,32},{32,48},{48,64},{64,80},{80,96},{96,112},{112,128},... | collective-permute-start | bytes 24584 | tf_op jit(solution)/shard_map/ppermute | solution.py:27
  137.0 29.0 %all_gather.38 = f32[128,4,32]{2,1,0:T(4,128)S(1)} all-gather(f32[4,4,32]{2,1,0:T(4,128)S(1)} %broadcast_multiply_fusion.6), channel_id=1, replica_groups=mesh['gx'=32,'gy'=16] {'gx'}, dimensions={0}, use_global_device_ids=true | all-gather | bytes 67584 | tf_op jit(solution)/shard_map/all_gather | solution.py:147
  168.1 6.4 %collective-permute-start.19 = (f32[18,1,128]{2,1,0:T(1,128)S(1)}, f32[18,1,128]{2,1,0:T(1,128)S(1)}, u32[]{:S(2)}, u32[]{:S(2)}) collective-permute-start(f32[18,1,128]{2,1,0:T(1,128)S(1)} %get-tuple-element.36), channel_id=1, source_target_pairs={{0,1},{1,2},{2,3},{3,4},{4,5},{5,6},{6,7},{7,8},{8,9},{9,10},{10,1... | collective-permute-start | bytes 27656 | tf_op jit(solution)/shard_map/ppermute | solution.py:27
  174.5 2.4 collective-permute-start.14
  176.9 1.5 collective-permute-start.15
  178.5 9.8 %reshape.37 = f32[8,2,8,2,64,2]{5,4,3,2,1,0:T(8,128)} reshape(f32[16,16,128]{2,1,0:T(8,128)S(1)} %copy-done.15) | data formatting | bytes 262144 | tf_op jit(solution)/shard_map/reshape | solution.py:99
  188.3 4.1 reduce_sum.162
  192.8 9.8 %reshape.41 = f32[8,2,8,2,64,2]{5,4,3,2,1,0:T(8,128)} reshape(f32[16,16,128]{2,1,0:T(8,128)S(1)} %fusion.77) | data formatting | bytes 262144 | tf_op jit(solution)/shard_map/reshape | solution.py:99
  202.6 4.0 reduce_sum.166
  206.7 1.9 collective-permute-start.20
  208.7 3.6 collective-permute-start.21
  214.4 7.0 %collective-permute-start.23 = (f32[10,1,64]{2,1,0:T(1,128)S(1)}, f32[10,1,64]{2,1,0:T(1,128)S(1)}, u32[]{:S(2)}, u32[]{:S(2)}) collective-permute-start(f32[10,1,64]{2,1,0:T(1,128)S(1)} %get-tuple-element.58), channel_id=1, source_target_pairs={{0,1},{1,2},{2,3},{3,4},{4,5},{5,6},{6,7},{7,8},{8,9},{9,10},{10,1... | collective-permute-start | bytes 7688 | tf_op jit(solution)/shard_map/ppermute | solution.py:27
  222.8 1.9 collective-permute-start.24
  224.7 4.5 %collective-permute-start.25 = (f32[1,8,64]{2,1,0:T(8,128)S(1)}, f32[1,8,64]{2,1,0:T(8,128)S(1)}, u32[]{:S(2)}, u32[]{:S(2)}) collective-permute-start(f32[1,8,64]{2,1,0:T(8,128)S(1)} %get-tuple-element.65), channel_id=1, source_target_pairs={{0,16},{16,32},{32,48},{48,64},{64,80},{80,96},{96,112},{112,128},... | collective-permute-start | bytes 6152 | tf_op jit(solution)/shard_map/ppermute | solution.py:27
  231.3 6.4 %collective-permute-start.27 = (f32[10,1,64]{2,1,0:T(1,128)S(1)}, f32[10,1,64]{2,1,0:T(1,128)S(1)}, u32[]{:S(2)}, u32[]{:S(2)}) collective-permute-start(f32[10,1,64]{2,1,0:T(1,128)S(1)} %get-tuple-element.56), channel_id=1, source_target_pairs={{0,1},{1,2},{2,3},{3,4},{4,5},{5,6},{6,7},{7,8},{8,9},{9,10},{10,1... | collective-permute-start | bytes 7688 | tf_op jit(solution)/shard_map/ppermute | solution.py:27
  237.7 32.7 %all_gather.32 = f32[128,4,32]{2,1,0:T(4,128)S(1)} all-gather(f32[4,4,32]{2,1,0:T(4,128)S(1)} %broadcast_multiply_fusion.9), channel_id=1, replica_groups=mesh['gx'=32,'gy'=16] {'gx'}, dimensions={0}, use_global_device_ids=true | all-gather | bytes 67584 | tf_op jit(solution)/shard_map/all_gather | solution.py:144
  271.5 2.1 collective-permute-start.28
  273.5 3.5 collective-permute-start.29
  279.1 6.7 %collective-permute-start.31 = (f32[10,1,64]{2,1,0:T(1,128)S(1)}, f32[10,1,64]{2,1,0:T(1,128)S(1)}, u32[]{:S(2)}, u32[]{:S(2)}) collective-permute-start(f32[10,1,64]{2,1,0:T(1,128)S(1)} %get-tuple-element.54), channel_id=1, source_target_pairs={{0,1},{1,2},{2,3},{3,4},{4,5},{5,6},{6,7},{7,8},{8,9},{9,10},{10,1... | collective-permute-start | bytes 7688 | tf_op jit(solution)/shard_map/ppermute | solution.py:27
  286.8 1.9 collective-permute-start.32
  288.7 5.0 %collective-permute-start.33 = (f32[1,8,64]{2,1,0:T(8,128)S(1)}, f32[1,8,64]{2,1,0:T(8,128)S(1)}, u32[]{:S(2)}, u32[]{:S(2)}) collective-permute-start(f32[1,8,64]{2,1,0:T(8,128)S(1)} %get-tuple-element.61), channel_id=1, source_target_pairs={{0,16},{16,32},{32,48},{48,64},{64,80},{80,96},{96,112},{112,128},... | collective-permute-start | bytes 6152 | tf_op jit(solution)/shard_map/ppermute | solution.py:27
  295.8 6.4 %collective-permute-start.35 = (f32[10,1,64]{2,1,0:T(1,128)S(1)}, f32[10,1,64]{2,1,0:T(1,128)S(1)}, u32[]{:S(2)}, u32[]{:S(2)}) collective-permute-start(f32[10,1,64]{2,1,0:T(1,128)S(1)} %get-tuple-element.52), channel_id=1, source_target_pairs={{0,1},{1,2},{2,3},{3,4},{4,5},{5,6},{6,7},{7,8},{8,9},{9,10},{10,1... | collective-permute-start | bytes 7688 | tf_op jit(solution)/shard_map/ppermute | solution.py:27
  304.4 33.5 %all_gather.30 = f32[128,4,32]{2,1,0:T(4,128)S(1)} all-gather(f32[4,4,32]{2,1,0:T(4,128)S(1)} %broadcast_multiply_fusion.10), channel_id=1, replica_groups=mesh['gx'=32,'gy'=16] {'gx'}, dimensions={0}, use_global_device_ids=true | all-gather | bytes 67584 | tf_op jit(solution)/shard_map/all_gather | solution.py:143
  338.6 2.6 slice.637
  341.3 2.2 slice.638
  343.5 2.5 slice.639
  346.0 56.3 %all-gather.6.cloned.1.call-done = f32[128,64,32]{0,2,1:T(8,128)} async-done(((f32[128,4,32]{0,2,1:T(8,128)}), f32[128,64,32]{0,2,1:T(8,128)}) %all-gather.6.cloned.1.call-update) | async-done | bytes 1048592 | tf_op jit(solution)/shard_map/all_gather | solution.py:150
  402.3 8.4 %multiply_reduce_fusion.6 = (f32[]{:T(128)}, f32[]{:T(128)}, f32[128,64,32]{0,2,1:T(8,128)}) fusion(f32[128,64,32]{0,2,1:T(8,128)} %all-gather.6.cloned.1.call-done, f32[128,64,32]{0,2,1:T(8,128)S(1)} %copy-done.2, f32[128,64,31]{0,2,1:T(8,128)} %slice.639, f32[128,64,32]{0,2,1:T(8,128)} %all-gather.12.cloned.1.call-done, f32[128,63,32]{0,2,1:T(8,128)} %slice.638, ...), kind=kLoop, calls=%fused_computation.106 | loop fusion | flops 6029310 | bytes 9379848 | tf_op jit(solution)/shard_map/reduce_sum | solution.py:117
  413.5 5.5 %multiply_reduce_fusion.4 = (f32[]{:T(128)}, f32[]{:T(128)}, f32[128,64,32]{0,2,1:T(8,128)}) fusion(f32[128,64,32]{0,2,1:T(8,128)S(1)} %multiply_subtract_fusion.2, f32[128,64,32]{0,2,1:T(8,128)} %all-gather.14.cloned.1.call-done, f32[128,64,31]{0,2,1:T(8,128)} %slice.639, f32[128,64,32]{0,2,1:T(8,128)} %all-gather.12.cloned.1.call-done, ...), kind=kLoop, calls=%fused_computation.103 | loop fusion | flops 6029310 | bytes 9379848 | tf_op jit(solution)/shard_map/reduce_sum | solution.py:120
  422.7 2.1 multiply_reduce_fusion.3
  426.2 2.2 multiply_add_fusion
  429.3 4.5 %multiply_reduce_fusion.2 = (f32[]{:T(128)}, f32[128,64,32]{0,2,1:T(8,128)}) fusion(f32[128,64,32]{0,2,1:T(8,128)S(1)} %copy-done, f32[128,64,32]{0,2,1:T(8,128)S(1)} %copy-done.3, f32[128,64,32]{0,2,1:T(8,128)S(1)} %multiply_add_fusion, f32[128,64,31]{0,2,1:T(8,128)S(1)} %copy-done.7, f32[128,64,32]{0,2,1:T(8,128)S(1)} %copy-done.10, ...), kind=kLoop, calls=%fused_computation.99 | loop fusion | flops 5505023 | bytes 10428420 | tf_op jit(solution)/shard_map/reduce_sum | solution.py:117
  435.2 2.1 multiply_subtract_fusion
  438.0 4.2 multiply_reduce_fusion
  (184 shorter events, 39.6 us)
Async XLA Ops:
  7.2 331.4 %all-gather.10.cloned.1.call-start = ((), (), s32[]{:S(2)}) async-start(), calls=%async_computation.2 | async-start | bytes 1114112 | tf_op jit(solution)/shard_map/all_gather | solution.py:152
  9.3 44.5 %copy-start.12 = (f32[16,16,128]{2,1,0:T(8,128)S(1)}, f32[16,16,128]{2,1,0:T(8,128)}, u32[]{:S(2)}) copy-start(f32[16,16,128]{2,1,0:T(8,128)} %param.9) | copy-start | bytes 393220
  9.6 46.1 %copy-start.15 = (f32[16,16,128]{2,1,0:T(8,128)S(1)}, f32[16,16,128]{2,1,0:T(8,128)}, u32[]{:S(2)}) copy-start(f32[16,16,128]{2,1,0:T(8,128)} %param.6) | copy-start | bytes 393220
  9.7 46.1 %copy-start.18 = (f32[16,16,128]{2,1,0:T(8,128)S(1)}, f32[16,16,128]{2,1,0:T(8,128)}, u32[]{:S(2)}) copy-start(f32[16,16,128]{2,1,0:T(8,128)} %param.5) | copy-start | bytes 393220
  49.0 292.3 %all-gather.12.cloned.1.call-start = ((), (), s32[]{:S(2)}) async-start(), calls=%async_computation.3 | async-start | bytes 1114112 | tf_op jit(solution)/shard_map/all_gather | solution.py:153
  49.1 5.4 %collective-permute-start = (f32[1,16,128]{2,1,0:T(8,128)S(1)}, f32[1,16,128]{2,1,0:T(8,128)S(1)}, u32[]{:S(2)}, u32[]{:S(2)}) collective-permute-start(f32[1,16,128]{2,1,0:T(8,128)S(1)} %slice.478), channel_id=1, source_target_pairs={{16,0},{32,16},{48,32},{64,48},{80,64},{96,80},{112,96},{128,112},... | collective-permute-start | bytes 24584 | tf_op jit(solution)/shard_map/ppermute | solution.py:16
  51.2 4.5 %collective-permute-start.1 = (f32[16,1,128]{2,1,0:T(1,128)S(1)}, f32[16,1,128]{2,1,0:T(1,128)S(1)}, u32[]{:S(2)}, u32[]{:S(2)}) collective-permute-start(f32[16,1,128]{2,1,0:T(1,128)S(1)} %slice.480), channel_id=1, source_target_pairs={{1,0},{2,1},{3,2},{4,3},{5,4},{6,5},{7,6},{8,7},{9,8},{10,9},{11,1... | collective-permute-start | bytes 24584 | tf_op jit(solution)/shard_map/ppermute | solution.py:16
  55.8 6.5 %collective-permute-start.2 = (f32[1,16,128]{2,1,0:T(8,128)S(1)}, f32[1,16,128]{2,1,0:T(8,128)S(1)}, u32[]{:S(2)}, u32[]{:S(2)}) collective-permute-start(f32[1,16,128]{2,1,0:T(8,128)S(1)} %get-tuple-element.51), channel_id=1, source_target_pairs={{16,0},{32,16},{48,32},{64,48},{80,64},{96,80},{112,96},{128,112},... | collective-permute-start | bytes 24584 | tf_op jit(solution)/shard_map/ppermute | solution.py:29
  58.2 4.9 %collective-permute-start.3 = (f32[1,16,128]{2,1,0:T(8,128)S(1)}, f32[1,16,128]{2,1,0:T(8,128)S(1)}, u32[]{:S(2)}, u32[]{:S(2)}) collective-permute-start(f32[1,16,128]{2,1,0:T(8,128)S(1)} %get-tuple-element.50), channel_id=1, source_target_pairs={{0,16},{16,32},{32,48},{48,64},{64,80},{80,96},{96,112},{112,128},... | collective-permute-start | bytes 24584 | tf_op jit(solution)/shard_map/ppermute | solution.py:27
  63.1 36.6 %collective-permute-start.4 = (f32[18,1,128]{2,1,0:T(1,128)S(1)}, f32[18,1,128]{2,1,0:T(1,128)S(1)}, u32[]{:S(2)}, u32[]{:S(2)}) collective-permute-start(f32[18,1,128]{2,1,0:T(1,128)S(1)} %get-tuple-element.43), channel_id=1, source_target_pairs={{1,0},{2,1},{3,2},{4,3},{5,4},{6,5},{7,6},{8,7},{9,8},{10,9},{11,1... | collective-permute-start | bytes 27656 | tf_op jit(solution)/shard_map/ppermute | solution.py:29
  64.4 35.4 %collective-permute-start.5 = (f32[18,1,128]{2,1,0:T(1,128)S(1)}, f32[18,1,128]{2,1,0:T(1,128)S(1)}, u32[]{:S(2)}, u32[]{:S(2)}) collective-permute-start(f32[18,1,128]{2,1,0:T(1,128)S(1)} %get-tuple-element.42), channel_id=1, source_target_pairs={{0,1},{1,2},{2,3},{3,4},{4,5},{5,6},{6,7},{7,8},{8,9},{9,10},{10,1... | collective-permute-start | bytes 27656 | tf_op jit(solution)/shard_map/ppermute | solution.py:27
  99.7 243.9 %all-gather.14.cloned.1.call-start = ((), (), s32[]{:S(2)}) async-start(), calls=%async_computation.4 | async-start | bytes 1114112 | tf_op jit(solution)/shard_map/all_gather | solution.py:154
  100.3 5.6 %collective-permute-start.6 = (f32[1,16,128]{2,1,0:T(8,128)S(1)}, f32[1,16,128]{2,1,0:T(8,128)S(1)}, u32[]{:S(2)}, u32[]{:S(2)}) collective-permute-start(f32[1,16,128]{2,1,0:T(8,128)S(1)} %get-tuple-element.49), channel_id=1, source_target_pairs={{16,0},{32,16},{48,32},{64,48},{80,64},{96,80},{112,96},{128,112},... | collective-permute-start | bytes 24584 | tf_op jit(solution)/shard_map/ppermute | solution.py:29
  102.3 4.3 collective-permute-start.7
  106.6 7.8 %collective-permute-start.8 = (f32[18,1,128]{2,1,0:T(1,128)S(1)}, f32[18,1,128]{2,1,0:T(1,128)S(1)}, u32[]{:S(2)}, u32[]{:S(2)}) collective-permute-start(f32[18,1,128]{2,1,0:T(1,128)S(1)} %get-tuple-element.41), channel_id=1, source_target_pairs={{1,0},{2,1},{3,2},{4,3},{5,4},{6,5},{7,6},{8,7},{9,8},{10,9},{11,1... | collective-permute-start | bytes 27656 | tf_op jit(solution)/shard_map/ppermute | solution.py:29
  107.9 6.5 %collective-permute-start.9 = (f32[18,1,128]{2,1,0:T(1,128)S(1)}, f32[18,1,128]{2,1,0:T(1,128)S(1)}, u32[]{:S(2)}, u32[]{:S(2)}) collective-permute-start(f32[18,1,128]{2,1,0:T(1,128)S(1)} %get-tuple-element.40), channel_id=1, source_target_pairs={{0,1},{1,2},{2,3},{3,4},{4,5},{5,6},{6,7},{7,8},{8,9},{9,10},{10,1... | collective-permute-start | bytes 27656 | tf_op jit(solution)/shard_map/ppermute | solution.py:27
  114.9 7.1 %collective-permute-start.10 = (f32[1,16,128]{2,1,0:T(8,128)S(1)}, f32[1,16,128]{2,1,0:T(8,128)S(1)}, u32[]{:S(2)}, u32[]{:S(2)}) collective-permute-start(f32[1,16,128]{2,1,0:T(8,128)S(1)} %get-tuple-element.47), channel_id=1, source_target_pairs={{16,0},{32,16},{48,32},{64,48},{80,64},{96,80},{112,96},{128,112},... | collective-permute-start | bytes 24584 | tf_op jit(solution)/shard_map/ppermute | solution.py:29
  116.9 5.5 %collective-permute-start.11 = (f32[1,16,128]{2,1,0:T(8,128)S(1)}, f32[1,16,128]{2,1,0:T(8,128)S(1)}, u32[]{:S(2)}, u32[]{:S(2)}) collective-permute-start(f32[1,16,128]{2,1,0:T(8,128)S(1)} %get-tuple-element.46), channel_id=1, source_target_pairs={{0,16},{16,32},{32,48},{48,64},{64,80},{80,96},{96,112},{112,128},... | collective-permute-start | bytes 24584 | tf_op jit(solution)/shard_map/ppermute | solution.py:27
  122.4 6.1 %collective-permute-start.12 = (f32[18,1,128]{2,1,0:T(1,128)S(1)}, f32[18,1,128]{2,1,0:T(1,128)S(1)}, u32[]{:S(2)}, u32[]{:S(2)}) collective-permute-start(f32[18,1,128]{2,1,0:T(1,128)S(1)} %get-tuple-element.39), channel_id=1, source_target_pairs={{1,0},{2,1},{3,2},{4,3},{5,4},{6,5},{7,6},{8,7},{9,8},{10,9},{11,1... | collective-permute-start | bytes 27656 | tf_op jit(solution)/shard_map/ppermute | solution.py:29
  123.7 5.6 %collective-permute-start.13 = (f32[18,1,128]{2,1,0:T(1,128)S(1)}, f32[18,1,128]{2,1,0:T(1,128)S(1)}, u32[]{:S(2)}, u32[]{:S(2)}) collective-permute-start(f32[18,1,128]{2,1,0:T(1,128)S(1)} %get-tuple-element.38), channel_id=1, source_target_pairs={{0,1},{1,2},{2,3},{3,4},{4,5},{5,6},{6,7},{7,8},{8,9},{9,10},{10,1... | collective-permute-start | bytes 27656 | tf_op jit(solution)/shard_map/ppermute | solution.py:27
  130.0 62.7 %copy-start.19 = (f32[16,16,128]{2,1,0:T(8,128)}, f32[16,16,128]{2,1,0:T(8,128)S(1)}, u32[]{:S(2)}) copy-start(f32[16,16,128]{2,1,0:T(8,128)S(1)} %fusion.99) | copy-start | bytes 393220
  130.0 36.8 %collective-permute-start.16 = (f32[1,16,128]{2,1,0:T(8,128)S(1)}, f32[1,16,128]{2,1,0:T(8,128)S(1)}, u32[]{:S(2)}, u32[]{:S(2)}) collective-permute-start(f32[1,16,128]{2,1,0:T(8,128)S(1)} %get-tuple-element.45), channel_id=1, source_target_pairs={{16,0},{32,16},{48,32},{64,48},{80,64},{96,80},{112,96},{128,112},... | collective-permute-start | bytes 24584 | tf_op jit(solution)/shard_map/ppermute | solution.py:29
  131.9 34.9 %collective-permute-start.17 = (f32[1,16,128]{2,1,0:T(8,128)S(1)}, f32[1,16,128]{2,1,0:T(8,128)S(1)}, u32[]{:S(2)}, u32[]{:S(2)}) collective-permute-start(f32[1,16,128]{2,1,0:T(8,128)S(1)} %get-tuple-element.44), channel_id=1, source_target_pairs={{0,16},{16,32},{32,48},{48,64},{64,80},{80,96},{96,112},{112,128},... | collective-permute-start | bytes 24584 | tf_op jit(solution)/shard_map/ppermute | solution.py:27
  166.7 179.3 %all-gather.8.cloned.1.call-start = ((), (), s32[]{:S(2)}) async-start(), calls=%async_computation.1 | async-start | bytes 1114112 | tf_op jit(solution)/shard_map/all_gather | solution.py:151
  166.8 25.5 %collective-permute-start.18 = (f32[18,1,128]{2,1,0:T(1,128)S(1)}, f32[18,1,128]{2,1,0:T(1,128)S(1)}, u32[]{:S(2)}, u32[]{:S(2)}) collective-permute-start(f32[18,1,128]{2,1,0:T(1,128)S(1)} %get-tuple-element.37), channel_id=1, source_target_pairs={{1,0},{2,1},{3,2},{4,3},{5,4},{6,5},{7,6},{8,7},{9,8},{10,9},{11,1... | collective-permute-start | bytes 27656 | tf_op jit(solution)/shard_map/ppermute | solution.py:29
  168.1 24.2 %collective-permute-start.19 = (f32[18,1,128]{2,1,0:T(1,128)S(1)}, f32[18,1,128]{2,1,0:T(1,128)S(1)}, u32[]{:S(2)}, u32[]{:S(2)}) collective-permute-start(f32[18,1,128]{2,1,0:T(1,128)S(1)} %get-tuple-element.36), channel_id=1, source_target_pairs={{0,1},{1,2},{2,3},{3,4},{4,5},{5,6},{6,7},{7,8},{8,9},{9,10},{10,1... | collective-permute-start | bytes 27656 | tf_op jit(solution)/shard_map/ppermute | solution.py:27
  174.5 32.1 %collective-permute-start.14 = (f32[1,8,64]{2,1,0:T(8,128)S(1)}, f32[1,8,64]{2,1,0:T(8,128)S(1)}, u32[]{:S(2)}, u32[]{:S(2)}) collective-permute-start(f32[1,8,64]{2,1,0:T(8,128)S(1)} %slice.613), channel_id=1, source_target_pairs={{16,0},{32,16},{48,32},{64,48},{80,64},{96,80},{112,96},{128,112},... | collective-permute-start | bytes 6152 | tf_op jit(solution)/shard_map/ppermute | solution.py:16
  176.9 29.8 %collective-permute-start.15 = (f32[8,1,64]{2,1,0:T(1,128)S(1)}, f32[8,1,64]{2,1,0:T(1,128)S(1)}, u32[]{:S(2)}, u32[]{:S(2)}) collective-permute-start(f32[8,1,64]{2,1,0:T(1,128)S(1)} %slice.615), channel_id=1, source_target_pairs={{1,0},{2,1},{3,2},{4,3},{5,4},{6,5},{7,6},{8,7},{9,8},{10,9},{11,1... | collective-permute-start | bytes 6152 | tf_op jit(solution)/shard_map/ppermute | solution.py:16
  206.7 5.6 %collective-permute-start.20 = (f32[1,8,64]{2,1,0:T(8,128)S(1)}, f32[1,8,64]{2,1,0:T(8,128)S(1)}, u32[]{:S(2)}, u32[]{:S(2)}) collective-permute-start(f32[1,8,64]{2,1,0:T(8,128)S(1)} %get-tuple-element.68), channel_id=1, source_target_pairs={{16,0},{32,16},{48,32},{64,48},{80,64},{96,80},{112,96},{128,112},... | collective-permute-start | bytes 6152 | tf_op jit(solution)/shard_map/ppermute | solution.py:29
  208.7 4.4 collective-permute-start.21
  213.1 9.5 %collective-permute-start.22 = (f32[10,1,64]{2,1,0:T(1,128)S(1)}, f32[10,1,64]{2,1,0:T(1,128)S(1)}, u32[]{:S(2)}, u32[]{:S(2)}) collective-permute-start(f32[10,1,64]{2,1,0:T(1,128)S(1)} %get-tuple-element.59), channel_id=1, source_target_pairs={{1,0},{2,1},{3,2},{4,3},{5,4},{6,5},{7,6},{8,7},{9,8},{10,9},{11,1... | collective-permute-start | bytes 7688 | tf_op jit(solution)/shard_map/ppermute | solution.py:29
  214.4 8.2 %collective-permute-start.23 = (f32[10,1,64]{2,1,0:T(1,128)S(1)}, f32[10,1,64]{2,1,0:T(1,128)S(1)}, u32[]{:S(2)}, u32[]{:S(2)}) collective-permute-start(f32[10,1,64]{2,1,0:T(1,128)S(1)} %get-tuple-element.58), channel_id=1, source_target_pairs={{0,1},{1,2},{2,3},{3,4},{4,5},{5,6},{6,7},{7,8},{8,9},{9,10},{10,1... | collective-permute-start | bytes 7688 | tf_op jit(solution)/shard_map/ppermute | solution.py:27
  222.8 6.5 %collective-permute-start.24 = (f32[1,8,64]{2,1,0:T(8,128)S(1)}, f32[1,8,64]{2,1,0:T(8,128)S(1)}, u32[]{:S(2)}, u32[]{:S(2)}) collective-permute-start(f32[1,8,64]{2,1,0:T(8,128)S(1)} %get-tuple-element.66), channel_id=1, source_target_pairs={{16,0},{32,16},{48,32},{64,48},{80,64},{96,80},{112,96},{128,112},... | collective-permute-start | bytes 6152 | tf_op jit(solution)/shard_map/ppermute | solution.py:29
  224.7 5.3 %collective-permute-start.25 = (f32[1,8,64]{2,1,0:T(8,128)S(1)}, f32[1,8,64]{2,1,0:T(8,128)S(1)}, u32[]{:S(2)}, u32[]{:S(2)}) collective-permute-start(f32[1,8,64]{2,1,0:T(8,128)S(1)} %get-tuple-element.65), channel_id=1, source_target_pairs={{0,16},{16,32},{32,48},{48,64},{64,80},{80,96},{96,112},{112,128},... | collective-permute-start | bytes 6152 | tf_op jit(solution)/shard_map/ppermute | solution.py:27
  230.0 41.2 %collective-permute-start.26 = (f32[10,1,64]{2,1,0:T(1,128)S(1)}, f32[10,1,64]{2,1,0:T(1,128)S(1)}, u32[]{:S(2)}, u32[]{:S(2)}) collective-permute-start(f32[10,1,64]{2,1,0:T(1,128)S(1)} %get-tuple-element.57), channel_id=1, source_target_pairs={{1,0},{2,1},{3,2},{4,3},{5,4},{6,5},{7,6},{8,7},{9,8},{10,9},{11,1... | collective-permute-start | bytes 7688 | tf_op jit(solution)/shard_map/ppermute | solution.py:29
  231.3 39.9 %collective-permute-start.27 = (f32[10,1,64]{2,1,0:T(1,128)S(1)}, f32[10,1,64]{2,1,0:T(1,128)S(1)}, u32[]{:S(2)}, u32[]{:S(2)}) collective-permute-start(f32[10,1,64]{2,1,0:T(1,128)S(1)} %get-tuple-element.56), channel_id=1, source_target_pairs={{0,1},{1,2},{2,3},{3,4},{4,5},{5,6},{6,7},{7,8},{8,9},{9,10},{10,1... | collective-permute-start | bytes 7688 | tf_op jit(solution)/shard_map/ppermute | solution.py:27
  271.2 131.2 %all-gather.6.cloned.1.call-start = ((), (), s32[]{:S(2)}) async-start(), calls=%async_computation | async-start | bytes 1114112 | tf_op jit(solution)/shard_map/all_gather | solution.py:150
  271.5 5.6 %collective-permute-start.28 = (f32[1,8,64]{2,1,0:T(8,128)S(1)}, f32[1,8,64]{2,1,0:T(8,128)S(1)}, u32[]{:S(2)}, u32[]{:S(2)}) collective-permute-start(f32[1,8,64]{2,1,0:T(8,128)S(1)} %get-tuple-element.64), channel_id=1, source_target_pairs={{16,0},{32,16},{48,32},{64,48},{80,64},{96,80},{112,96},{128,112},... | collective-permute-start | bytes 6152 | tf_op jit(solution)/shard_map/ppermute | solution.py:29
  273.5 4.2 collective-permute-start.29
  277.8 8.0 %collective-permute-start.30 = (f32[10,1,64]{2,1,0:T(1,128)S(1)}, f32[10,1,64]{2,1,0:T(1,128)S(1)}, u32[]{:S(2)}, u32[]{:S(2)}) collective-permute-start(f32[10,1,64]{2,1,0:T(1,128)S(1)} %get-tuple-element.55), channel_id=1, source_target_pairs={{1,0},{2,1},{3,2},{4,3},{5,4},{6,5},{7,6},{8,7},{9,8},{10,9},{11,1... | collective-permute-start | bytes 7688 | tf_op jit(solution)/shard_map/ppermute | solution.py:29
  279.1 7.4 %collective-permute-start.31 = (f32[10,1,64]{2,1,0:T(1,128)S(1)}, f32[10,1,64]{2,1,0:T(1,128)S(1)}, u32[]{:S(2)}, u32[]{:S(2)}) collective-permute-start(f32[10,1,64]{2,1,0:T(1,128)S(1)} %get-tuple-element.54), channel_id=1, source_target_pairs={{0,1},{1,2},{2,3},{3,4},{4,5},{5,6},{6,7},{7,8},{8,9},{9,10},{10,1... | collective-permute-start | bytes 7688 | tf_op jit(solution)/shard_map/ppermute | solution.py:27
  286.7 54.5 %copy-start.20 = (f32[8,8,64]{2,1,0:T(8,128)}, f32[8,8,64]{2,1,0:T(8,128)S(1)}, u32[]{:S(2)}) copy-start(f32[8,8,64]{2,1,0:T(8,128)S(1)} %fusion.186) | copy-start | bytes 49156
  286.8 7.0 %collective-permute-start.32 = (f32[1,8,64]{2,1,0:T(8,128)S(1)}, f32[1,8,64]{2,1,0:T(8,128)S(1)}, u32[]{:S(2)}, u32[]{:S(2)}) collective-permute-start(f32[1,8,64]{2,1,0:T(8,128)S(1)} %get-tuple-element.62), channel_id=1, source_target_pairs={{16,0},{32,16},{48,32},{64,48},{80,64},{96,80},{112,96},{128,112},... | collective-permute-start | bytes 6152 | tf_op jit(solution)/shard_map/ppermute | solution.py:29
  288.7 5.8 %collective-permute-start.33 = (f32[1,8,64]{2,1,0:T(8,128)S(1)}, f32[1,8,64]{2,1,0:T(8,128)S(1)}, u32[]{:S(2)}, u32[]{:S(2)}) collective-permute-start(f32[1,8,64]{2,1,0:T(8,128)S(1)} %get-tuple-element.61), channel_id=1, source_target_pairs={{0,16},{16,32},{32,48},{48,64},{64,80},{80,96},{96,112},{112,128},... | collective-permute-start | bytes 6152 | tf_op jit(solution)/shard_map/ppermute | solution.py:27
  294.5 7.7 %collective-permute-start.34 = (f32[10,1,64]{2,1,0:T(1,128)S(1)}, f32[10,1,64]{2,1,0:T(1,128)S(1)}, u32[]{:S(2)}, u32[]{:S(2)}) collective-permute-start(f32[10,1,64]{2,1,0:T(1,128)S(1)} %get-tuple-element.53), channel_id=1, source_target_pairs={{1,0},{2,1},{3,2},{4,3},{5,4},{6,5},{7,6},{8,7},{9,8},{10,9},{11,1... | collective-permute-start | bytes 7688 | tf_op jit(solution)/shard_map/ppermute | solution.py:29
  295.8 7.1 %collective-permute-start.35 = (f32[10,1,64]{2,1,0:T(1,128)S(1)}, f32[10,1,64]{2,1,0:T(1,128)S(1)}, u32[]{:S(2)}, u32[]{:S(2)}) collective-permute-start(f32[10,1,64]{2,1,0:T(1,128)S(1)} %get-tuple-element.52), channel_id=1, source_target_pairs={{0,1},{1,2},{2,3},{3,4},{4,5},{5,6},{6,7},{7,8},{8,9},{9,10},{10,1... | collective-permute-start | bytes 7688 | tf_op jit(solution)/shard_map/ppermute | solution.py:27
  338.6 63.7 %copy-start.1 = (f32[128,64,32]{0,2,1:T(8,128)S(1)}, f32[128,64,32]{0,2,1:T(8,128)}, u32[]{:S(2)}) copy-start(f32[128,64,32]{0,2,1:T(8,128)} %all-gather.10.cloned.1.call-done) | copy-start | bytes 3145732
  343.5 58.8 %copy-start.2 = (f32[128,64,32]{0,2,1:T(8,128)S(1)}, f32[128,64,32]{0,2,1:T(8,128)}, u32[]{:S(2)}) copy-start(f32[128,64,32]{0,2,1:T(8,128)} %all-gather.14.cloned.1.call-done) | copy-start | bytes 3145732
  (14 other events, 126.8 us)
Sparse Core Ops, SparseCore 0:
  49.1 52.0 all-gather.9
  104.3 57.3 all-gather.11
  166.9 63.0 all-gather.13
  271.3 62.7 all-gather.7
  338.7 63.5 all-gather.5
where the time goes:
time: 454 us; the launch traced here: 452 us
  blocking collectives  164 us (36%)
  starting transfers between devices  113 us (25%)
  waiting for transfers between devices  64.7 us (14%)
  other arithmetic  45.4 us (10%)
  local copies, waits for them, and re-layouts  40.3 us (9%)
  between operations  24 us (5%)
    ppermute x16, starting transfers between devices, extended(): lax.ppermute(tail, axis, [(i, (i + 1) % count) for i in range(ends)])  79.6 us
    all_gather x1, waiting for transfers between devices, per_device(): lax.all_gather(pieces[0], 'gy', axis=1, tiled=True)  56.3 us
    all_gather x1, blocking collectives, per_device(): lax.all_gather(bx, 'gx', axis=0, tiled=True)  38.3 us
    all_gather x1, blocking collectives, per_device(): lax.all_gather(rhs, 'gx', axis=0, tiled=True)  33.5 us
    all_gather x1, blocking collectives, per_device(): lax.all_gather(alpha, 'gx', axis=0, tiled=True)  32.7 us
    all_gather x1, blocking collectives, per_device(): lax.all_gather(by, 'gx', axis=0, tiled=True)  30.5 us
    all_gather x1, blocking collectives, per_device(): lax.all_gather(bz, 'gx', axis=0, tiled=True)  29 us
    ppermute x16, starting transfers between devices, extended(): lax.ppermute(head, axis, [((i + 1) % count, i) for i in range(ends)])  26.4 us
  transfers between devices with their start and end apart: 41, of which 12 were waited for; matrix products, arithmetic and copies ran while one was open for 11% of the time, Pallas kernels for 0%

commit v1 on v0

v1 whole, which is shorter than its diff:
```python
import jax
import jax.numpy as jnp
from jax import lax
from jax.experimental import pallas as pl
from jax.experimental.pallas import tpu as pltpu
from jax.sharding import PartitionSpec as P

MESH = pl.DeviceIdType.MESH
F32 = jnp.float32

BICG = 2
LMAX = 2.0
LMIN = 0.25
THETA = 0.5 * (LMAX + LMIN)
DELTA = 0.5 * (LMAX - LMIN)
SIGMA = THETA / DELTA

HALO = 4
LANES = 128
DIRECTIONS = ((1, 1), (1, -1), (-1, 1), (-1, -1), (0, 1), (0, -1), (1, 0), (-1, 0))
SHRINK = 0.125


def steps():
    rho = 1.0 / SIGMA
    out = []
    for _ in range(3):
        rho_next = 1.0 / (2.0 * SIGMA - rho)
        out.append((rho_next * rho, 2.0 * rho_next / DELTA))
        rho = rho_next
    return out


def lane_of(shape):
    return lax.broadcasted_iota(jnp.int32, shape, len(shape) - 1)


def roll(value, shift, axis):
    extent = value.shape[axis]
    return pltpu.roll(value, shift % extent, axis)


def spans(offset, own):
    if offset == 1:
        return pl.ds(own, HALO), pl.ds(0, HALO)
    if offset == -1:
        return pl.ds(HALO, HALO), pl.ds(own + HALO, HALO)
    return pl.ds(HALO, own), pl.ds(HALO, own)


def kernel(
    nx, ny,
    rhs_hbm, alpha_hbm, bx_hbm, by_hbm, bz_hbm,
    fine_hbm, one_ref, bottom_ref,
    raw, ext0, work0, pair0,
    raw1, packed1, coef1, work1, rhs1, pair1,
    packed2, coef2, basis,
    gather_y, gather_x,
    load_sem, out_sem, send_sem, recv_sem, ysend, yrecv, xsend, xrecv,
):
    gx = lax.axis_index("gx")
    gy = lax.axis_index("gy")
    n0, n1, n2 = raw.shape[1], raw1.shape[1], raw1.shape[1] // 2

    loads = [
        pltpu.make_async_copy(src, raw.at[i], load_sem.at[i])
        for i, src in enumerate((rhs_hbm, alpha_hbm, bx_hbm, by_hbm, bz_hbm))
    ]
    for copy in loads:
        copy.start()

    def has(dx, dy):
        ok = None
        for step, at, count in ((dx, gx, nx), (dy, gy, ny)):
            if step != 0:
                this = at < count - 1 if step > 0 else at > 0
                ok = this if ok is None else jnp.logical_and(ok, this)
        return ok

    barrier = pltpu.get_barrier_semaphore()
    greeted = jnp.int32(nx - 1 + ny - 1)
    for dx, dy in DIRECTIONS[:4]:
        there = has(dx, dy)
        greeted = greeted + there.astype(jnp.int32)

        @pl.when(there)
        def _(dx=dx, dy=dy):
            pl.semaphore_signal(barrier, inc=1, device_id=(gx + dx, gy + dy), device_id_type=MESH)

    def peer_y(o):
        return (gx, lax.rem(gy + o, ny))

    def peer_x(o):
        return (lax.rem(gx + o, nx), gy)

    for o in range(1, nx):
        pl.semaphore_signal(barrier, inc=1, device_id=peer_x(o), device_id_type=MESH)
    for o in range(1, ny):
        pl.semaphore_signal(barrier, inc=1, device_id=peer_y(o), device_id_type=MESH)

    def exchange(which, ref, own, lead):
        out = []
        for j, (dx, dy) in enumerate(DIRECTIONS):
            (sx, tx), (sy, ty) = spans(dx, own), spans(dy, own)
            src, dst = (ref.at[:, sx, sy], ref.at[:, tx, ty]) if lead else (ref.at[sx, sy], ref.at[tx, ty])
            copy = pltpu.make_async_remote_copy(
                src, dst, send_sem.at[which, j], recv_sem.at[which, j],
                device_id=(gx + dx, gy + dy), device_id_type=MESH,
            )
            out.append((copy, has(dx, dy), has(-dx, -dy)))
        return out

    def start(copies):
        for copy, to, _ in copies:
            pl.when(to)(copy.start)

    def arrive(copies):
        for copy, _, of in copies:
            pl.when(of)(copy.wait_recv)

    def leave(copies):
        for copy, to, _ in copies:
            pl.when(to)(copy.wait_send)

    x_inner = jnp.where(gx > 0, 1.0, 0.0).astype(F32)

    def own_coefs(alpha, bx, by, bz, scale, width):
        n = bx.shape[0]
        col = lax.broadcasted_iota(jnp.int32, bx.shape, 1)
        bz_in = jnp.where(lane_of(bx.shape) < width, 0.0, bz)
        bxu = jnp.concatenate([bx[1:], jnp.zeros_like(bx[:1])], 0)
        byu = jnp.where(col == n - 1, 0.0, roll(by, -1, 1))
        diag = alpha + scale * (bx + bxu + by + byu + bz + roll(bz_in, -width, 2))
        by_in = jnp.where(jnp.logical_and(col == 0, gy == 0), 0.0, by)
        bx_in = jnp.concatenate([bx[:1] * x_inner, bx[1:]], 0)
        return diag, bx_in, by_in, bz_in

    for copy in loads:
        copy.wait()

    own = pl.ds(HALO, n0)
    diag, bx_in, by_in, bz_in = own_coefs(raw[1], raw[2], raw[3], raw[4], 16.0, 1)
    for i, v in enumerate((raw[0], diag, bx_in, by_in, bz_in)):
        ext0[i, own, own, :] = v

    pl.semaphore_wait(barrier, greeted)
    sent0 = exchange(0, ext0, n0, True)
    start(sent0)

    def halves(ref, n):
        return ref[:, pl.ds(0, n, stride=2), :], ref[:, pl.ds(1, n, stride=2), :]

    def coarsen(alpha, bx, by, bz, pairs, width):
        n = bx.shape[0] // 2

        def xs(v):
            w = v.reshape((n, 2) + v.shape[1:])
            return w[:, 0], w[:, 1]

        def zsum(v):
            return v + roll(v, -width, 2)

        pairs[0, :, pl.ds(0, 2 * n)] = zsum(sum(xs(alpha)))
        pairs[1, :, pl.ds(0, 2 * n)] = zsum(xs(bx)[0])
        pairs[2, :, pl.ds(0, 2 * n)] = zsum(sum(xs(by)))
        pairs[3, :, pl.ds(0, 2 * n)] = sum(xs(bz))
        a0, a1 = halves(pairs.at[0], n)
        x0, x1 = halves(pairs.at[1], n)
        y0, _ = halves(pairs.at[2], n)
        z0, z1 = halves(pairs.at[3], n)
        return (a0 + a1) * 0.125, (x0 + x1) * 0.25, y0 * 0.25, (z0 + z1) * 0.25

    alpha1, bx1, by1, bz1 = coarsen(raw[1], raw[2], raw[3], raw[4], pair0, 1)
    diag, bx_in, by_in, bz_in = own_coefs(alpha1, bx1, by1, bz1, 4.0, 2)
    own = pl.ds(HALO, n1)
    lane = lane_of(diag.shape)
    packed1[0, own, own, :] = jnp.where(lane % 2 == 0, diag, roll(bx_in, 1, 2))
    packed1[1, own, own, :] = jnp.where(lane % 2 == 0, by_in, roll(bz_in, 1, 2))
    sent1 = exchange(1, packed1, n1, True)
    start(sent1)

    alpha2, bx2, by2, bz2 = coarsen(alpha1, bx1, by1, bz1, pair1, 2)
    diag, bx_in, by_in, bz_in = own_coefs(alpha2, bx2, by2, bz2, 1.0, 4)
    own = pl.ds(HALO, n2)
    lane = lane_of(diag.shape) % 4
    mixed = jnp.where(lane < 2, jnp.where(lane == 0, diag, roll(bx_in, 1, 2)), jnp.where(lane == 2, roll(by_in, 2, 2), roll(bz_in, 3, 2)))
    packed2[own, own, :] = mixed
    sent2 = exchange(2, packed2, n2, False)
    start(sent2)

    def border(ref, index, n, value):
        for flag, at in ((gx == 0, 0), (gx == nx - 1, n + HALO)):

            @pl.when(flag)
            def _(at=at):
                ref[index + (pl.ds(at, HALO),)] = value((HALO, n + 2 * HALO, LANES))

        for flag, at in ((gy == 0, 0), (gy == ny - 1, n + HALO)):

            @pl.when(flag)
            def _(at=at):
                ref[index + (slice(None), pl.ds(at, HALO))] = value((n + 2 * HALO, HALO, LANES))

    def zeros(shape):
        return jnp.zeros(shape, F32)

    def ones(every):
        return lambda shape: jnp.where(lane_of(shape) % every == 0, 1.0, 0.0).astype(F32)

    for i in (0, 2, 3, 4):
        border(ext0, (i,), n0, zeros)
    border(ext0, (1,), n0, ones(1))
    border(packed1, (0,), n1, ones(2))
    border(packed1, (1,), n1, zeros)
    border(rhs1, (), n1, zeros)

    def border2(ref, value):
        for flag, at in ((gx == 0, 0), (gx == nx - 1, n2 + HALO)):

            @pl.when(flag)
            def _(at=at):
                ref[pl.ds(at, HALO)] = value((HALO,) + ref.shape[1:])

        for flag, at in ((gy == 0, 0), (gy == ny - 1, n2 + HALO)):

            @pl.when(flag)
            def _(at=at):
                ref[:, pl.ds(at, HALO)] = value((ref.shape[0], HALO, LANES))

    border2(packed2, ones(4))
    border2(basis.at[0], zeros)

    def whole_diag(part, bx, by, n, scale):
        rows = part.shape[0]
        row = lax.broadcasted_iota(jnp.int32, part.shape, 0)
        col = lax.broadcasted_iota(jnp.int32, part.shape, 1)
        at_x = jnp.logical_or(row == HALO - 1, row == HALO + n - 1)
        at_y = jnp.logical_or(col == HALO - 1, col == HALO + n - 1)
        bxu = jnp.concatenate([bx[1:rows], jnp.zeros_like(bx[:1])], 0)
        return part + scale * (jnp.where(at_x, bxu, 0.0) + jnp.where(at_y, roll(by, -1, 1), 0.0))

    def sweep(number, faces, work, n, width, finish):
        coefs = steps()
        first, last = number + 1, n + 2 * HALO - number - 1
        rows = {22: 2, 20: 4, 18: 6, 16: 4, 14: 7, 12: 6, 10: 5, 8: 4}[last - first]
        source, target = 6 + number % 2, 7 - number % 2

        def body(i, carry):
            at = first + i * rows
            here = pl.ds(at, rows)
            x = work[source, here]
            total = faces[0, here] * work[source, pl.ds(at - 1, rows)]
            total = total + faces[0, pl.ds(at + 1, rows)] * work[source, pl.ds(at + 1, rows)]
            total = total + faces[1, here] * roll(x, 1, 1) + work[2, here] * roll(x, -1, 1)
            total = total + faces[2, here] * roll(x, width, 2) + work[3, here] * roll(x, -width, 2)
            scaled = work[1, here] - x + work[0, here] * total
            if number == 3:
                finish(at, rows, work[4, here] * scaled)
            else:
                a, b = coefs[number]
                update = a * (x if number == 0 else work[5, here]) + b * scaled
                work[5, here] = update
                work[target, here] = x + update
            return carry

        lax.fori_loop(0, (last - first) // rows, body, 0)

    def smooth(faces, work, n, width, finish):
        for number in range(4):
            sweep(number, faces, work, n, width, finish)

    def prepare(faces, work, diag, scale, width):
        inverse = 1.0 / diag
        work[0] = scale * inverse
        work[2] = roll(faces[1], -1, 1)
        work[3] = roll(faces[2], -width, 2)
        work[4] = diag

    def begin(work, rhs, scale):
        work[1] = work[0] * rhs * (1.0 / scale)
        work[6] = work[1] * (1.0 / THETA)

    arrive(sent0)
    faces0 = ext0.at[pl.ds(2, 3)]
    prepare(faces0, work0, whole_diag(ext0[1], ext0[2], ext0[3], n0, 16.0), 16.0, 1)
    begin(work0, ext0[0], 16.0)

    def halve(pairs, width):
        def finish(at, rows, resid):
            summed = resid.reshape((rows // 2, 2) + resid.shape[1:])
            summed = summed[:, 0] + summed[:, 1]
            half = lax.div(at - HALO, 2)
            pairs[pl.ds(half, rows // 2)] = summed + roll(summed, -width, 2)

        return finish

    def restrict(pairs, n):
        even = pairs[:, pl.ds(HALO, n, stride=2), :]
        odd = pairs[:, pl.ds(HALO + 1, n, stride=2), :]
        return (even + odd) * 0.125

    down0 = pair0.at[4]
    smooth(faces0, work0, n0, 1, halve(down0, 1))
    own = pl.ds(HALO, n1)
    rhs1[own, own, :] = restrict(down0, n1)
    sent3 = exchange(3, rhs1, n1, False)
    start(sent3)

    own = pl.ds(HALO, n0)
    store = pltpu.make_async_copy(work0.at[7, own, own], fine_hbm, out_sem)
    store.start()

    arrive(sent1)
    even = lane_of(packed1.shape[1:]) % 2 == 0
    part = jnp.where(even, packed1[0], 1.0)
    coef1[0] = roll(packed1[0], -1, 2)
    coef1[1] = packed1[1]
    coef1[2] = roll(packed1[1], -1, 2)
    prepare(coef1, work1, whole_diag(part, coef1[0], coef1[1], n1, 4.0), 4.0, 2)

    arrive(sent2)
    mixed = packed2[...] * SHRINK
    bx_in, by_in, bz_in = roll(mixed, -1, 2), roll(mixed, -2, 2), roll(mixed, -3, 2)
    coef2[0] = whole_diag(mixed, bx_in, by_in, n2, 1.0)
    coef2[1] = bx_in
    coef2[2] = by_in
    coef2[3] = roll(by_in, -1, 1)
    coef2[4] = bz_in
    coef2[5] = roll(bz_in, -4, 2)

    arrive(sent3)
    begin(work1, rhs1[...], 4.0)
    down1 = pair1.at[4]
    smooth(coef1, work1, n1, 2, halve(down1, 2))
    own = pl.ds(HALO, n2)
    basis[0, own, own, :] = restrict(down1, n2)
    sent4 = exchange(4, basis.at[0], n2, False)
    start(sent4)

    def compacted(value, width):
        rows = value.reshape((-1, LANES))
        count = LANES // width
        pick = lax.broadcasted_iota(jnp.int32, (LANES, count), 0) == width * lax.broadcasted_iota(jnp.int32, (LANES, count), 1)
        out = jnp.dot(rows, pick.astype(F32), precision=lax.Precision.HIGHEST, preferred_element_type=F32)
        return out.reshape(value.shape[:-1] + (count,))

    own = pl.ds(HALO, n1)
    one_ref[...] = compacted(work1[7, own, own, :], 2)

    arrive(sent4)
    for number in range(4):
        first, last = number + 1, n2 + 2 * HALO - number - 1
        here = pl.ds(first, last - first)
        x = basis[number, here]
        total = coef2[1, here] * basis[number, pl.ds(first - 1, last - first)]
        total = total + coef2[1, pl.ds(first + 1, last - first)] * basis[number, pl.ds(first + 1, last - first)]
        total = total + coef2[2, here] * roll(x, 1, 1) + coef2[3, here] * roll(x, -1, 1)
        total = total + coef2[4, here] * roll(x, 4, 2) + coef2[5, here] * roll(x, -4, 2)
        basis[number + 1, here] = coef2[0, here] * x - total

    own = pl.ds(HALO, n2)
    vectors = [basis[i, own, own, :] for i in range(5)]
    valid = lane_of((n2, LANES)) % 4 == 0
    lane = lane_of((1, LANES))
    row = jnp.zeros((1, LANES), F32)
    for k in range(9):
        product = jnp.sum(vectors[k // 2] * vectors[(k + 1) // 2], axis=0)
        product = jnp.where(valid, product, 0.0)
        moment = jnp.sum(jnp.sum(product, axis=0, keepdims=True), axis=1, keepdims=True)
        row = jnp.where(lane == k, moment, row)

    def all_sum(row, slots, ssem, rsem, peer):
        slots[0] = row
        copies = [
            pltpu.make_async_remote_copy(slots.at[0], slots.at[o], ssem.at[o], rsem.at[o], device_id=peer(o), device_id_type=MESH)
            for o in range(1, slots.shape[0])
        ]
        for copy in copies:
            copy.start()
        for copy in copies:
            copy.wait_recv()
        return jnp.sum(slots[...], axis=0), copies

    row, sent5 = all_sum(row, gather_y, ysend, yrecv, peer_y)
    row, sent6 = all_sum(row, gather_x, xsend, xrecv, peer_x)
    moments = [jnp.sum(jnp.where(lane == k, row, 0.0), axis=1, keepdims=True) for k in range(9)]

    def inner(u, w):
        total = None
        for i, a in enumerate(u):
            for j, b in enumerate(w):
                if a is not None and b is not None:
                    term = a * b * moments[i + j]
                    total = term if total is None else total + term
        return total

    def plus(u, c, w):
        out = []
        for a, b in zip(u, w):
            term = None if b is None else c * b
            out.append(a if term is None else term if a is None else a + term)
        return out

    def applied(u):
        return [None] + [None if a is None else a * (1.0 / SHRINK) for a in u[:-1]]

    shadow = [jnp.ones((1, 1), F32), None, None, None, None]
    solved = [None] * 5
    resid = direction = shadow
    rho = moments[0]
    for number in range(BICG):
        image = applied(direction)
        step = rho / inner(shadow, image)
        half = plus(resid, -step, image)
        turned = applied(half)
        omega = inner(turned, half) / inner(turned, turned)
        solved = plus(plus(solved, step, direction), omega, half)
        if number + 1 < BICG:
            resid = plus(half, -omega, turned)
            rho_next = inner(shadow, resid)
            factor = (rho_next / rho) * (step / omega)
            direction = plus(resid, factor, plus(direction, -omega, image))
            rho = rho_next

    total = None
    for i, c in enumerate(solved):
        if c is not None:
            term = c * basis[i, pl.ds(HALO, n2), pl.ds(0, 2 * HALO), :]
            total = term if total is None else total + term
    bottom_ref[...] = compacted(total, 4)[:, HALO:, :]

    for copies in (sent0, sent1, sent2, sent3, sent4):
        leave(copies)
    for copy in sent5 + sent6:
        copy.wait_send()
    store.wait()


def per_device(right_side, alpha_cells, beta_x, beta_y, beta_z):
    nx, ny = lax.axis_size("gx"), lax.axis_size("gy")
    n0, _, nz = right_side.shape
    n1, n2 = n0 // 2, n0 // 4
    e0, e1, e2 = n0 + 2 * HALO, n1 + 2 * HALO, n2 + 2 * HALO
    anywhere = pl.BlockSpec(memory_space=pl.ANY)
    vmem = pl.BlockSpec(memory_space=pltpu.VMEM)

    def body(*refs):
        kernel(nx, ny, *refs)

    return pl.pallas_call(
        body,
        out_shape=(
            jax.ShapeDtypeStruct((n0, n0, nz), F32),
            jax.ShapeDtypeStruct((n1, n1, nz // 2), F32),
            jax.ShapeDtypeStruct((n2, n2, nz // 4), F32),
        ),
        in_specs=[anywhere] * 5,
        out_specs=(anywhere, vmem, vmem),
        scratch_shapes=[
            pltpu.VMEM((5, n0, n0, nz), F32),
            pltpu.VMEM((5, e0, e0, nz), F32),
            pltpu.VMEM((8, e0, e0, nz), F32),
            pltpu.VMEM((5, n1, e0, nz), F32),
            pltpu.VMEM((4, n1, n1, nz), F32),
            pltpu.VMEM((2, e1, e1, nz), F32),
            pltpu.VMEM((3, e1, e1, nz), F32),
            pltpu.VMEM((8, e1, e1, nz), F32),
            pltpu.VMEM((e1, e1, nz), F32),
            pltpu.VMEM((5, n2, e1, nz), F32),
            pltpu.VMEM((e2, 16, nz), F32),
            pltpu.VMEM((6, e2, 16, nz), F32),
            pltpu.VMEM((5, e2, 16, nz), F32),
            pltpu.VMEM((ny, 1, nz), F32),
            pltpu.VMEM((nx, 1, nz), F32),
            pltpu.SemaphoreType.DMA((5,)),
            pltpu.SemaphoreType.DMA,
            pltpu.SemaphoreType.DMA((5, 8)),
            pltpu.SemaphoreType.DMA((5, 8)),
            pltpu.SemaphoreType.DMA((ny,)),
            pltpu.SemaphoreType.DMA((ny,)),
            pltpu.SemaphoreType.DMA((nx,)),
            pltpu.SemaphoreType.DMA((nx,)),
        ],
        compiler_params=pltpu.CompilerParams(collective_id=0, has_side_effects=True, vmem_limit_bytes=32 * 2**20),
        cost_estimate=pl.CostEstimate(flops=40_000_000, bytes_accessed=800_000, transcendentals=0),
        name="vcycle_down",
    )(right_side, alpha_cells, beta_x, beta_y, beta_z)


def solution(mesh):
    placed = P("gx", "gy", None)
    return jax.shard_map(per_device, mesh=mesh, in_specs=(placed,) * 5, out_specs=(placed,) * 3, check_vma=False)
```

time: 454 us -> 60.1 us (0.13)
  blocking collectives: 164 us -> 0 us
  starting transfers between devices: 113 us -> 0 us
  waiting for transfers between devices: 64.7 us -> 0 us
  Pallas kernels: 0 us -> 52.8 us
  other arithmetic: 45.4 us -> 0 us
  local copies, waits for them, and re-layouts: 40.3 us -> 6.38 us
  between operations: 24 us -> 0.65 us
    all_gather x5 -> x0, blocking collectives: 164 us -> none  [the longest x1 38.3 us: per_device(): lax.all_gather(bx, 'gx', axis=0, tiled=True)]
    ppermute x36 -> x0, starting transfers between devices: 113 us -> none  [the longest x16 79.6 us: extended(): lax.ppermute(tail, axis, [(i, (i + 1) % count) for i in range(ends)])]
    all_gather x5 -> x0, waiting for transfers between devices: 56.3 us -> none  [the longest x1 56.3 us: per_device(): lax.all_gather(pieces[0], 'gy', axis=1, tiled=True)]
    pallas_call x0 -> x1, Pallas kernels: none -> 52.8 us  [per_device(): pl.pallas_call(body, out_shape=(jax.ShapeDtypeStruct((n0, n0, nz), F32),...]
    reduce_sum x15 -> x0, other arithmetic: 35.4 us -> none  [the longest x2 12.9 us: whole_bicgstab(): step = rho / jnp.sum(rhs * image)]
    reshape x3 -> x0, local copies, waits for them, and re-layouts: 20.7 us -> none  [restrict_cells(): return values.reshape(a // 2, 2, b // 2, 2, c // 2, 2).mean(axis=(1, 3, 5))]
    slice x31 -> x0, local copies, waits for them, and re-layouts: 12.2 us -> none  [the longest x5 7.5 us: next_face(): head = lax.slice_in_dim(coeff, 1, count, axis=axis)]
    ppermute x36 -> x0, waiting for transfers between devices: 8.3 us -> none  [the longest x16 7.01 us: extended(): lax.ppermute(tail, axis, [(i, (i + 1) % count) for i in range(ends)])]
  transfers between devices with their start and end apart: 41 -> 0, of which waited for: 12 -> 0; matrix products, arithmetic and copies ran while one was open for 11% -> 0% of each run, Pallas kernels for 0% -> 0%
where the time goes in v1:
time: 60.1 us; the launch traced here: 59.9 us
  Pallas kernels  52.8 us (88%)
  local copies, waits for them, and re-layouts  6.38 us (11%)
  between operations  0.65 us (1%)
    pallas_call x1, Pallas kernels, per_device(): pl.pallas_call(body, out_shape=(jax.ShapeDtypeStruct((n0, n0, nz), F32),...  52.8 us
    unnamed x13, local copies, waits for them, and re-layouts  6.38 us

profile of v1, /device:TPU:1, one launch (start us, length us, event | category | flops | bytes accessed | tf_op | source)
XLA Modules:
  0.0 59.9 jit_solution(17667284604570215313)
XLA Ops:
  0.6 0.0 copy-start
  0.6 0.9 %copy-done = f32[16,16,128]{2,1,0:T(8,128)S(1)} copy-done((f32[16,16,128]{2,1,0:T(8,128)S(1)}, f32[16,16,128]{2,1,0:T(8,128)}, u32[]{:S(2)}) %copy-start) | copy-done | bytes 131096
  1.5 0.0 copy-start.1
  1.5 0.9 %copy-done.1 = f32[16,16,128]{2,1,0:T(8,128)S(1)} copy-done((f32[16,16,128]{2,1,0:T(8,128)S(1)}, f32[16,16,128]{2,1,0:T(8,128)}, u32[]{:S(2)}) %copy-start.1) | copy-done | bytes 131096
  2.4 0.0 copy-start.2
  2.4 0.9 %copy-done.2 = f32[16,16,128]{2,1,0:T(8,128)S(1)} copy-done((f32[16,16,128]{2,1,0:T(8,128)S(1)}, f32[16,16,128]{2,1,0:T(8,128)}, u32[]{:S(2)}) %copy-start.2) | copy-done | bytes 131096
  3.3 0.0 copy-start.3
  3.3 0.9 %copy-done.3 = f32[16,16,128]{2,1,0:T(8,128)S(1)} copy-done((f32[16,16,128]{2,1,0:T(8,128)S(1)}, f32[16,16,128]{2,1,0:T(8,128)}, u32[]{:S(2)}) %copy-start.3) | copy-done | bytes 131096
  4.3 0.0 copy-start.4
  4.3 0.9 %copy-done.4 = f32[16,16,128]{2,1,0:T(8,128)S(1)} copy-done((f32[16,16,128]{2,1,0:T(8,128)S(1)}, f32[16,16,128]{2,1,0:T(8,128)}, u32[]{:S(2)}) %copy-start.4) | copy-done | bytes 131096
  5.2 52.8 %vcycle_down.1 = (f32[16,16,128]{2,1,0:T(8,128)S(1)}, f32[8,8,64]{2,1,0:T(8,128)S(1)}, f32[4,4,32]{2,1,0:T(4,128)S(1)}) custom-call(f32[16,16,128]{2,1,0:T(8,128)S(1)} %copy-done, f32[16,16,128]{2,1,0:T(8,128)S(1)} %copy-done.1, f32[16,16,128]{2,1,0:T(8,128)S(1)} %copy-done.2, f32[16,16,128]{2,1,0:T(8,128)S(1)} %copy-done.3, f32[16,16,128]{2,1,0:T(8,128)S(1)} %copy-done.4), custom_call_target="tpu_custom_call" | custom-call | flops 40000000 | bytes 800000 | tf_op jit(solution)/shard_map/vcycle_down/pallas_call | solution.py:450
  58.0 0.7 %copy.11 = f32[16,16,128]{2,1,0:T(8,128)} copy(f32[16,16,128]{2,1,0:T(8,128)S(1)} %get-tuple-element.6) | data formatting | bytes 262144
  58.7 0.6 %copy.12 = f32[8,8,64]{2,1,0:T(8,128)} copy(f32[8,8,64]{2,1,0:T(8,128)S(1)} %get-tuple-element.7) | data formatting | bytes 32768
  59.3 0.6 copy.13
Async XLA Ops:
  0.6 0.9 %copy-start = (f32[16,16,128]{2,1,0:T(8,128)S(1)}, f32[16,16,128]{2,1,0:T(8,128)}, u32[]{:S(2)}) copy-start(f32[16,16,128]{2,1,0:T(8,128)} %refs_0_.1) | copy-start | bytes 393220
  1.5 0.9 %copy-start.1 = (f32[16,16,128]{2,1,0:T(8,128)S(1)}, f32[16,16,128]{2,1,0:T(8,128)}, u32[]{:S(2)}) copy-start(f32[16,16,128]{2,1,0:T(8,128)} %refs_1_.1) | copy-start | bytes 393220
  2.4 0.9 %copy-start.2 = (f32[16,16,128]{2,1,0:T(8,128)S(1)}, f32[16,16,128]{2,1,0:T(8,128)}, u32[]{:S(2)}) copy-start(f32[16,16,128]{2,1,0:T(8,128)} %refs_2_.1) | copy-start | bytes 393220
  3.3 0.9 %copy-start.3 = (f32[16,16,128]{2,1,0:T(8,128)S(1)}, f32[16,16,128]{2,1,0:T(8,128)}, u32[]{:S(2)}) copy-start(f32[16,16,128]{2,1,0:T(8,128)} %refs_3_.1) | copy-start | bytes 393220
  4.3 0.9 %copy-start.4 = (f32[16,16,128]{2,1,0:T(8,128)S(1)}, f32[16,16,128]{2,1,0:T(8,128)}, u32[]{:S(2)}) copy-start(f32[16,16,128]{2,1,0:T(8,128)} %refs_4_.1) | copy-start | bytes 393220

commit v2 on v1

--- a/solution.py
+++ b/solution.py
@@ -40,23 +40,23 @@
     return pltpu.roll(value, shift % extent, axis)
 
 
-def spans(offset, own):
+def spans(offset, own, depth=HALO, skip=0):
     if offset == 1:
-        return pl.ds(own, HALO), pl.ds(0, HALO)
+        return pl.ds(own + HALO - skip - depth, depth), pl.ds(HALO - skip - depth, depth)
     if offset == -1:
-        return pl.ds(HALO, HALO), pl.ds(own + HALO, HALO)
+        return pl.ds(HALO + skip, depth), pl.ds(own + HALO + skip, depth)
     return pl.ds(HALO, own), pl.ds(HALO, own)
 
 
 def kernel(
     nx, ny,
     rhs_hbm, alpha_hbm, bx_hbm, by_hbm, bz_hbm,
-    fine_hbm, one_ref, bottom_ref,
+    fine_hbm, one_hbm, bottom_hbm,
     raw, ext0, work0, pair0,
     raw1, packed1, coef1, work1, rhs1, pair1,
     packed2, coef2, basis,
-    gather_y, gather_x,
-    load_sem, out_sem, send_sem, recv_sem, ysend, yrecv, xsend, xrecv,
+    gather_y, gather_x, one_ref, bottom_ref,
+    load_sem, out_sem, send_sem, recv_sem, more_send, more_recv, row_send, row_recv, known_x, known_y,
 ):
     gx = lax.axis_index("gx")
     gy = lax.axis_index("gy")
@@ -78,7 +78,7 @@
         return ok
 
     barrier = pltpu.get_barrier_semaphore()
-    greeted = jnp.int32(nx - 1 + ny - 1)
+    greeted = jnp.int32(4)
     for dx, dy in DIRECTIONS[:4]:
         there = has(dx, dy)
         greeted = greeted + there.astype(jnp.int32)
@@ -88,27 +88,64 @@
             pl.semaphore_signal(barrier, inc=1, device_id=(gx + dx, gy + dy), device_id_type=MESH)
 
     def peer_y(o):
-        return (gx, lax.rem(gy + o, ny))
+        return (gx, lax.rem(gy + o + ny, ny))
 
     def peer_x(o):
-        return (lax.rem(gx + o, nx), gy)
-
-    for o in range(1, nx):
+        return (lax.rem(gx + o + nx, nx), gy)
+
+    for o in (1, -1):
         pl.semaphore_signal(barrier, inc=1, device_id=peer_x(o), device_id_type=MESH)
-    for o in range(1, ny):
         pl.semaphore_signal(barrier, inc=1, device_id=peer_y(o), device_id_type=MESH)
 
-    def exchange(which, ref, own, lead):
+    def tell(number):
+        for sems, peer, count in ((known_x, peer_x, nx), (known_y, peer_y, ny)):
+            if 2**number < count // 2:
+                for o in (2**number, -(2**number)):
+                    pl.semaphore_signal(sems.at[number], inc=1, device_id=peer(o), device_id_type=MESH)
+
+    def told(number):
+        for sems, count in ((known_x, nx), (known_y, ny)):
+            if 2**number < count // 2:
+                pl.semaphore_wait(sems.at[number], 2)
+
+    def remote(src, dst, ssem, rsem, dx, dy):
+        copy = pltpu.make_async_remote_copy(src, dst, ssem, rsem, device_id=(gx + dx, gy + dy), device_id_type=MESH)
+        return copy, has(dx, dy), has(-dx, -dy)
+
+    def exchange(which, ref, own, lead, corner=HALO, skip=()):
         out = []
         for j, (dx, dy) in enumerate(DIRECTIONS):
-            (sx, tx), (sy, ty) = spans(dx, own), spans(dy, own)
+            if (dx, dy) in skip:
+                continue
+            depth = corner if dx * dy != 0 else HALO
+            (sx, tx), (sy, ty) = spans(dx, own, depth), spans(dy, own, depth)
             src, dst = (ref.at[:, sx, sy], ref.at[:, tx, ty]) if lead else (ref.at[sx, sy], ref.at[tx, ty])
-            copy = pltpu.make_async_remote_copy(
-                src, dst, send_sem.at[which, j], recv_sem.at[which, j],
-                device_id=(gx + dx, gy + dy), device_id_type=MESH,
-            )
-            out.append((copy, has(dx, dy), has(-dx, -dy)))
+            out.append(remote(src, dst, send_sem.at[which, j], recv_sem.at[which, j], dx, dy))
         return out
+
+    def exchange_fine(ref, own):
+        out = exchange(0, ref, own, True, HALO - 1, ((0, 1), (0, -1)))
+        corners, sides = out[:4], out[4:]
+        more = []
+
+        def add(src, dst, dx, dy):
+            k = len(more)
+            more.append(remote(src, dst, more_send.at[k], more_recv.at[k], dx, dy))
+
+        for dx, dy in DIRECTIONS[:4]:
+            if dy == -1:
+                (sx, tx), (sy, ty) = spans(dx, own, 1, HALO - 1), spans(dy, own, 1)
+                add(ref.at[0, sx, sy], ref.at[0, tx, ty], dx, dy)
+            if dx == -1:
+                (sx, tx), (sy, ty) = spans(dx, own, 1), spans(dy, own, 1, HALO - 1)
+                add(ref.at[3, sx, sy], ref.at[3, tx, ty], dx, dy)
+        whole = pl.ds(HALO, own)
+        for dy in (1, -1):
+            sy, ty = spans(dy, own)
+            add(ref.at[pl.ds(0, 3), whole, sy], ref.at[pl.ds(0, 3), whole, ty], 0, dy)
+            sy, ty = spans(dy, own, HALO - 1)
+            add(ref.at[pl.ds(3, 2), whole, sy], ref.at[pl.ds(3, 2), whole, ty], 0, dy)
+        return corners + more + sides
 
     def start(copies):
         for copy, to, _ in copies:
@@ -140,12 +177,13 @@
 
     own = pl.ds(HALO, n0)
     diag, bx_in, by_in, bz_in = own_coefs(raw[1], raw[2], raw[3], raw[4], 16.0, 1)
-    for i, v in enumerate((raw[0], diag, bx_in, by_in, bz_in)):
+    for i, v in enumerate((by_in, raw[0], diag, bx_in, bz_in)):
         ext0[i, own, own, :] = v
 
     pl.semaphore_wait(barrier, greeted)
-    sent0 = exchange(0, ext0, n0, True)
+    sent0 = exchange_fine(ext0, n0)
     start(sent0)
+    tell(0)
 
     def halves(ref, n):
         return ref[:, pl.ds(0, n, stride=2), :], ref[:, pl.ds(1, n, stride=2), :]
@@ -207,9 +245,9 @@
     def ones(every):
         return lambda shape: jnp.where(lane_of(shape) % every == 0, 1.0, 0.0).astype(F32)
 
-    for i in (0, 2, 3, 4):
+    for i in (0, 1, 3, 4):
         border(ext0, (i,), n0, zeros)
-    border(ext0, (1,), n0, ones(1))
+    border(ext0, (2,), n0, ones(1))
     border(packed1, (0,), n1, ones(2))
     border(packed1, (1,), n1, zeros)
     border(rhs1, (), n1, zeros)
@@ -249,10 +287,10 @@
             at = first + i * rows
             here = pl.ds(at, rows)
             x = work[source, here]
-            total = faces[0, here] * work[source, pl.ds(at - 1, rows)]
-            total = total + faces[0, pl.ds(at + 1, rows)] * work[source, pl.ds(at + 1, rows)]
-            total = total + faces[1, here] * roll(x, 1, 1) + work[2, here] * roll(x, -1, 1)
-            total = total + faces[2, here] * roll(x, width, 2) + work[3, here] * roll(x, -width, 2)
+            total = faces[0][here] * work[source, pl.ds(at - 1, rows)]
+            total = total + faces[0][pl.ds(at + 1, rows)] * work[source, pl.ds(at + 1, rows)]
+            total = total + faces[1][here] * roll(x, 1, 1) + work[2, here] * roll(x, -1, 1)
+            total = total + faces[2][here] * roll(x, width, 2) + work[3, here] * roll(x, -width, 2)
             scaled = work[1, here] - x + work[0, here] * total
             if number == 3:
                 finish(at, rows, work[4, here] * scaled)
@@ -263,7 +301,7 @@
                 work[target, here] = x + update
             return carry
 
-        lax.fori_loop(0, (last - first) // rows, body, 0)
+        lax.fori_loop(0, (last - first) // rows, body, 0, unroll=True)
 
     def smooth(faces, work, n, width, finish):
         for number in range(4):
@@ -272,8 +310,8 @@
     def prepare(faces, work, diag, scale, width):
         inverse = 1.0 / diag
         work[0] = scale * inverse
-        work[2] = roll(faces[1], -1, 1)
-        work[3] = roll(faces[2], -width, 2)
+        work[2] = roll(faces[1][...], -1, 1)
+        work[3] = roll(faces[2][...], -width, 2)
         work[4] = diag
 
     def begin(work, rhs, scale):
@@ -281,9 +319,11 @@
         work[6] = work[1] * (1.0 / THETA)
 
     arrive(sent0)
-    faces0 = ext0.at[pl.ds(2, 3)]
-    prepare(faces0, work0, whole_diag(ext0[1], ext0[2], ext0[3], n0, 16.0), 16.0, 1)
-    begin(work0, ext0[0], 16.0)
+    told(0)
+    tell(1)
+    faces0 = (ext0.at[3], ext0.at[0], ext0.at[4])
+    prepare(faces0, work0, whole_diag(ext0[2], ext0[3], ext0[0], n0, 16.0), 16.0, 1)
+    begin(work0, ext0[1], 16.0)
 
     def halve(pairs, width):
         def finish(at, rows, resid):
@@ -303,11 +343,11 @@
     smooth(faces0, work0, n0, 1, halve(down0, 1))
     own = pl.ds(HALO, n1)
     rhs1[own, own, :] = restrict(down0, n1)
-    sent3 = exchange(3, rhs1, n1, False)
+    sent3 = exchange(3, rhs1, n1, False, HALO - 1)
     start(sent3)
 
     own = pl.ds(HALO, n0)
-    store = pltpu.make_async_copy(work0.at[7, own, own], fine_hbm, out_sem)
+    store = pltpu.make_async_copy(work0.at[7, own, own], fine_hbm, out_sem.at[0])
     store.start()
 
     arrive(sent1)
@@ -316,7 +356,8 @@
     coef1[0] = roll(packed1[0], -1, 2)
     coef1[1] = packed1[1]
     coef1[2] = roll(packed1[1], -1, 2)
-    prepare(coef1, work1, whole_diag(part, coef1[0], coef1[1], n1, 4.0), 4.0, 2)
+    faces1 = (coef1.at[0], coef1.at[1], coef1.at[2])
+    prepare(faces1, work1, whole_diag(part, coef1[0], coef1[1], n1, 4.0), 4.0, 2)
 
     arrive(sent2)
     mixed = packed2[...] * SHRINK
@@ -329,12 +370,14 @@
     coef2[5] = roll(bz_in, -4, 2)
 
     arrive(sent3)
+    told(1)
+    tell(2)
     begin(work1, rhs1[...], 4.0)
     down1 = pair1.at[4]
-    smooth(coef1, work1, n1, 2, halve(down1, 2))
+    smooth(faces1, work1, n1, 2, halve(down1, 2))
     own = pl.ds(HALO, n2)
     basis[0, own, own, :] = restrict(down1, n2)
-    sent4 = exchange(4, basis.at[0], n2, False)
+    sent4 = exchange(4, basis.at[0], n2, False, HALO - 1)
     start(sent4)
 
     def compacted(value, width):
@@ -346,8 +389,12 @@
 
     own = pl.ds(HALO, n1)
     one_ref[...] = compacted(work1[7, own, own, :], 2)
+    store_one = pltpu.make_async_copy(one_ref, one_hbm, out_sem.at[1])
+    store_one.start()
 
     arrive(sent4)
+    told(2)
+    tell(3)
     for number in range(4):
         first, last = number + 1, n2 + 2 * HALO - number - 1
         here = pl.ds(first, last - first)
@@ -369,20 +416,20 @@
         moment = jnp.sum(jnp.sum(product, axis=0, keepdims=True), axis=1, keepdims=True)
         row = jnp.where(lane == k, moment, row)
 
-    def all_sum(row, slots, ssem, rsem, peer):
+    def all_sum(row, slots, k, peer):
         slots[0] = row
-        copies = [
-            pltpu.make_async_remote_copy(slots.at[0], slots.at[o], ssem.at[o], rsem.at[o], device_id=peer(o), device_id_type=MESH)
-            for o in range(1, slots.shape[0])
-        ]
-        for copy in copies:
-            copy.start()
-        for copy in copies:
-            copy.wait_recv()
-        return jnp.sum(slots[...], axis=0), copies
-
-    row, sent5 = all_sum(row, gather_y, ysend, yrecv, peer_y)
-    row, sent6 = all_sum(row, gather_x, xsend, xrecv, peer_x)
+        count = slots.shape[0] - 1
+        for o in range(1, count + 1):
+            pltpu.make_async_remote_copy(
+                slots.at[0], slots.at[o], row_send.at[k], row_recv.at[k], device_id=peer(o), device_id_type=MESH
+            ).start()
+        others = slots.at[pl.ds(1, count)]
+        pltpu.make_async_copy(others, others, row_recv.at[k]).wait()
+        return jnp.sum(slots[...], axis=0), pltpu.make_async_copy(others, others, row_send.at[k])
+
+    row, sent5 = all_sum(row, gather_y, 0, peer_y)
+    told(3)
+    row, sent6 = all_sum(row, gather_x, 1, peer_x)
     moments = [jnp.sum(jnp.where(lane == k, row, 0.0), axis=1, keepdims=True) for k in range(9)]
 
     def inner(u, w):
@@ -428,12 +475,13 @@
             term = c * basis[i, pl.ds(HALO, n2), pl.ds(0, 2 * HALO), :]
             total = term if total is None else total + term
     bottom_ref[...] = compacted(total, 4)[:, HALO:, :]
+    store_bottom = pltpu.make_async_copy(bottom_ref, bottom_hbm, out_sem.at[2])
+    store_bottom.start()
 
     for copies in (sent0, sent1, sent2, sent3, sent4):
         leave(copies)
-    for copy in sent5 + sent6:
-        copy.wait_send()
-    store.wait()
+    for copy in (sent5, sent6, store, store_one, store_bottom):
+        copy.wait()
 
 
 def per_device(right_side, alpha_cells, beta_x, beta_y, beta_z):
@@ -442,7 +490,6 @@
     n1, n2 = n0 // 2, n0 // 4
     e0, e1, e2 = n0 + 2 * HALO, n1 + 2 * HALO, n2 + 2 * HALO
     anywhere = pl.BlockSpec(memory_space=pl.ANY)
-    vmem = pl.BlockSpec(memory_space=pltpu.VMEM)
 
     def body(*refs):
         kernel(nx, ny, *refs)
@@ -455,7 +502,7 @@
             jax.ShapeDtypeStruct((n2, n2, nz // 4), F32),
         ),
         in_specs=[anywhere] * 5,
-        out_specs=(anywhere, vmem, vmem),
+        out_specs=(anywhere,) * 3,
         scratch_shapes=[
             pltpu.VMEM((5, n0, n0, nz), F32),
             pltpu.VMEM((5, e0, e0, nz), F32),
@@ -472,16 +519,20 @@
             pltpu.VMEM((5, e2, 16, nz), F32),
             pltpu.VMEM((ny, 1, nz), F32),
             pltpu.VMEM((nx, 1, nz), F32),
+            pltpu.VMEM((n1, n1, nz // 2), F32),
+            pltpu.VMEM((n2, n2, nz // 4), F32),
             pltpu.SemaphoreType.DMA((5,)),
-            pltpu.SemaphoreType.DMA,
+            pltpu.SemaphoreType.DMA((3,)),
             pltpu.SemaphoreType.DMA((5, 8)),
             pltpu.SemaphoreType.DMA((5, 8)),
-            pltpu.SemaphoreType.DMA((ny,)),
-            pltpu.SemaphoreType.DMA((ny,)),
-            pltpu.SemaphoreType.DMA((nx,)),
-            pltpu.SemaphoreType.DMA((nx,)),
+            pltpu.SemaphoreType.DMA((8,)),
+            pltpu.SemaphoreType.DMA((8,)),
+            pltpu.SemaphoreType.DMA((2,)),
+            pltpu.SemaphoreType.DMA((2,)),
+            pltpu.SemaphoreType.REGULAR((4,)),
+            pltpu.SemaphoreType.REGULAR((4,)),
         ],
-        compiler_params=pltpu.CompilerParams(collective_id=0, has_side_effects=True, vmem_limit_bytes=32 * 2**20),
+        compiler_params=pltpu.CompilerParams(collective_id=0, has_side_effects=True, vmem_limit_bytes=60 * 2**20),
         cost_estimate=pl.CostEstimate(flops=40_000_000, bytes_accessed=800_000, transcendentals=0),
         name="vcycle_down",
     )(right_side, alpha_cells, beta_x, beta_y, beta_z)

time: 60.1 us -> 50.8 us (0.85)
  Pallas kernels: 52.8 us -> 47 us
  local copies, waits for them, and re-layouts: 6.38 us -> 2.88 us
    pallas_call x1, Pallas kernels: 52.8 us -> 47 us  [per_device(): pl.pallas_call(body, out_shape=(jax.ShapeDtypeStruct((n0, n0, nz), F32),...]
    unnamed x13 -> x7, local copies, waits for them, and re-layouts: 6.38 us -> 2.88 us
where the time goes in v2:
time: 50.8 us; the launch traced here: 50.6 us
  Pallas kernels  47 us (93%)
  local copies, waits for them, and re-layouts  2.88 us (6%)
  between operations  0.65 us (1%)
    pallas_call x1, Pallas kernels, per_device(): pl.pallas_call(body, out_shape=(jax.ShapeDtypeStruct((n0, n0, nz), F32),...  47 us
    unnamed x7, local copies, waits for them, and re-layouts  2.88 us

profile of v2, /device:TPU:1, one launch (start us, length us, event | category | flops | bytes accessed | tf_op | source)
XLA Modules:
  0.0 50.6 jit_solution(16246937585069853523)
XLA Ops:
  0.6 47.0 %vcycle_down.1 = (f32[16,16,128]{2,1,0:T(8,128)}, f32[8,8,64]{2,1,0:T(8,128)}, f32[4,4,32]{2,1,0:T(4,128)}) custom-call(f32[16,16,128]{2,1,0:T(8,128)} %refs_0_.1, f32[16,16,128]{2,1,0:T(8,128)} %refs_1_.1, f32[16,16,128]{2,1,0:T(8,128)} %refs_2_.1, f32[16,16,128]{2,1,0:T(8,128)} %refs_3_.1, f32[16,16,128]{2,1,0:T(8,128)} %refs_4_.1), custom_call_target="tpu_custom_call" | custom-call | flops 40000000 | bytes 800000 | tf_op jit(solution)/shard_map/vcycle_down/pallas_call | solution.py:497
  47.7 0.0 copy-start
  47.7 1.6 %copy.11 = f32[16,16,128]{2,1,0:T(8,128)} copy(f32[16,16,128]{2,1,0:T(8,128)} %get-tuple-element.6) | data formatting | bytes 262144
  49.3 0.0 copy-done
  49.3 0.0 copy-start.1
  49.3 0.6 %copy.12 = f32[8,8,64]{2,1,0:T(8,128)} copy(f32[8,8,64]{2,1,0:T(8,128)S(1)} %copy-done) | data formatting | bytes 32768
  49.9 0.1 copy-done.1
  50.0 0.6 %copy.13 = f32[4,4,32]{2,1,0:T(4,128)} copy(f32[4,4,32]{2,1,0:T(4,128)S(1)} %copy-done.1) | data formatting | bytes 4096
Async XLA Ops:
  47.7 1.6 %copy-start = (f32[8,8,64]{2,1,0:T(8,128)S(1)}, f32[8,8,64]{2,1,0:T(8,128)}, u32[]{:S(2)}) copy-start(f32[8,8,64]{2,1,0:T(8,128)} %get-tuple-element.7) | copy-start | bytes 49156
  49.3 0.7 %copy-start.1 = (f32[4,4,32]{2,1,0:T(4,128)S(1)}, f32[4,4,32]{2,1,0:T(4,128)}, u32[]{:S(2)}) copy-start(f32[4,4,32]{2,1,0:T(4,128)} %get-tuple-element.8) | copy-start | bytes 6148

commit v3 on v2

--- a/solution.py
+++ b/solution.py
@@ -51,23 +51,19 @@
 def kernel(
     nx, ny,
     rhs_hbm, alpha_hbm, bx_hbm, by_hbm, bz_hbm,
-    fine_hbm, one_hbm, bottom_hbm,
+    fine_ref, one_ref, bottom_ref,
     raw, ext0, work0, pair0,
     raw1, packed1, coef1, work1, rhs1, pair1,
     packed2, coef2, basis,
-    gather_y, gather_x, one_ref, bottom_ref,
+    gather_y, gather_x,
     load_sem, out_sem, send_sem, recv_sem, more_send, more_recv, row_send, row_recv, known_x, known_y,
 ):
     gx = lax.axis_index("gx")
     gy = lax.axis_index("gy")
     n0, n1, n2 = raw.shape[1], raw1.shape[1], raw1.shape[1] // 2
 
-    loads = [
-        pltpu.make_async_copy(src, raw.at[i], load_sem.at[i])
-        for i, src in enumerate((rhs_hbm, alpha_hbm, bx_hbm, by_hbm, bz_hbm))
-    ]
-    for copy in loads:
-        copy.start()
+    for i, src in enumerate((rhs_hbm, alpha_hbm, bx_hbm, by_hbm, bz_hbm)):
+        pltpu.make_async_copy(src, raw.at[i], load_sem).start()
 
     def has(dx, dy):
         ok = None
@@ -172,8 +168,7 @@
         bx_in = jnp.concatenate([bx[:1] * x_inner, bx[1:]], 0)
         return diag, bx_in, by_in, bz_in
 
-    for copy in loads:
-        copy.wait()
+    pltpu.make_async_copy(raw, raw, load_sem).wait()
 
     own = pl.ds(HALO, n0)
     diag, bx_in, by_in, bz_in = own_coefs(raw[1], raw[2], raw[3], raw[4], 16.0, 1)
@@ -347,7 +342,7 @@
     start(sent3)
 
     own = pl.ds(HALO, n0)
-    store = pltpu.make_async_copy(work0.at[7, own, own], fine_hbm, out_sem.at[0])
+    store = pltpu.make_async_copy(work0.at[7, own, own], fine_ref, out_sem)
     store.start()
 
     arrive(sent1)
@@ -389,8 +384,6 @@
 
     own = pl.ds(HALO, n1)
     one_ref[...] = compacted(work1[7, own, own, :], 2)
-    store_one = pltpu.make_async_copy(one_ref, one_hbm, out_sem.at[1])
-    store_one.start()
 
     arrive(sent4)
     told(2)
@@ -419,7 +412,7 @@
     def all_sum(row, slots, k, peer):
         slots[0] = row
         count = slots.shape[0] - 1
-        for o in range(1, count + 1):
+        for o in sorted(range(1, count + 1), key=lambda o: -min(o, count + 1 - o)):
             pltpu.make_async_remote_copy(
                 slots.at[0], slots.at[o], row_send.at[k], row_recv.at[k], device_id=peer(o), device_id_type=MESH
             ).start()
@@ -475,12 +468,10 @@
             term = c * basis[i, pl.ds(HALO, n2), pl.ds(0, 2 * HALO), :]
             total = term if total is None else total + term
     bottom_ref[...] = compacted(total, 4)[:, HALO:, :]
-    store_bottom = pltpu.make_async_copy(bottom_ref, bottom_hbm, out_sem.at[2])
-    store_bottom.start()
 
     for copies in (sent0, sent1, sent2, sent3, sent4):
         leave(copies)
-    for copy in (sent5, sent6, store, store_one, store_bottom):
+    for copy in (sent5, sent6, store):
         copy.wait()
 
 
@@ -490,6 +481,7 @@
     n1, n2 = n0 // 2, n0 // 4
     e0, e1, e2 = n0 + 2 * HALO, n1 + 2 * HALO, n2 + 2 * HALO
     anywhere = pl.BlockSpec(memory_space=pl.ANY)
+    vmem = pl.BlockSpec(memory_space=pltpu.VMEM)
 
     def body(*refs):
         kernel(nx, ny, *refs)
@@ -497,12 +489,12 @@
     return pl.pallas_call(
         body,
         out_shape=(
-            jax.ShapeDtypeStruct((n0, n0, nz), F32),
-            jax.ShapeDtypeStruct((n1, n1, nz // 2), F32),
-            jax.ShapeDtypeStruct((n2, n2, nz // 4), F32),
+            pltpu.VMEM((n0, n0, nz), F32),
+            pltpu.VMEM((n1, n1, nz // 2), F32),
+            pltpu.VMEM((n2, n2, nz // 4), F32),
         ),
         in_specs=[anywhere] * 5,
-        out_specs=(anywhere,) * 3,
+        out_specs=(vmem,) * 3,
         scratch_shapes=[
             pltpu.VMEM((5, n0, n0, nz), F32),
             pltpu.VMEM((5, e0, e0, nz), F32),
@@ -519,10 +511,8 @@
             pltpu.VMEM((5, e2, 16, nz), F32),
             pltpu.VMEM((ny, 1, nz), F32),
             pltpu.VMEM((nx, 1, nz), F32),
-            pltpu.VMEM((n1, n1, nz // 2), F32),
-            pltpu.VMEM((n2, n2, nz // 4), F32),
-            pltpu.SemaphoreType.DMA((5,)),
-            pltpu.SemaphoreType.DMA((3,)),
+            pltpu.SemaphoreType.DMA,
+            pltpu.SemaphoreType.DMA,
             pltpu.SemaphoreType.DMA((5, 8)),
             pltpu.SemaphoreType.DMA((5, 8)),
             pltpu.SemaphoreType.DMA((8,)),

time: 50.8 us -> 49 us (0.965)
  local copies, waits for them, and re-layouts: 2.88 us -> 1.87 us
  Pallas kernels: 47 us -> 46.3 us
    unnamed x7 -> x3, local copies, waits for them, and re-layouts: 2.88 us -> 1.87 us
    pallas_call x1, Pallas kernels: 47 us -> 46.3 us  [per_device(): pl.pallas_call(body, out_shape=(pltpu.VMEM((n0, n0, nz), F32), pltpu.VMEM...]
where the time goes in v3:
time: 49 us; the launch traced here: 48.8 us
  Pallas kernels  46.3 us (94%)
  local copies, waits for them, and re-layouts  1.87 us (4%)
  between operations  0.64 us (1%)
    pallas_call x1, Pallas kernels, per_device(): pl.pallas_call(body, out_shape=(pltpu.VMEM((n0, n0, nz), F32), pltpu.VMEM...  46.3 us
    unnamed x3, local copies, waits for them, and re-layouts  1.87 us

profile of v3, /device:TPU:1, one launch (start us, length us, event | category | flops | bytes accessed | tf_op | source)
XLA Modules:
  0.0 48.8 jit_solution(6514495437591387157)
XLA Ops:
  0.6 46.3 %vcycle_down.1 = (f32[16,16,128]{2,1,0:T(8,128)S(1)}, f32[8,8,64]{2,1,0:T(8,128)S(1)}, f32[4,4,32]{2,1,0:T(4,128)S(1)}) custom-call(f32[16,16,128]{2,1,0:T(8,128)} %refs_0_.1, f32[16,16,128]{2,1,0:T(8,128)} %refs_1_.1, f32[16,16,128]{2,1,0:T(8,128)} %refs_2_.1, f32[16,16,128]{2,1,0:T(8,128)} %refs_3_.1, f32[16,16,128]{2,1,0:T(8,128)} %refs_4_.1), custom_call_target="tpu_custom_call" | custom-call | flops 40000000 | bytes 800000 | tf_op jit(solution)/shard_map/vcycle_down/pallas_call | solution.py:489
  46.9 0.7 %copy.11 = f32[16,16,128]{2,1,0:T(8,128)} copy(f32[16,16,128]{2,1,0:T(8,128)S(1)} %get-tuple-element.3) | data formatting | bytes 262144
  47.6 0.6 %copy.13 = f32[4,4,32]{2,1,0:T(4,128)} copy(f32[4,4,32]{2,1,0:T(4,128)S(1)} %get-tuple-element.5) | data formatting | bytes 4096
  48.2 0.6 %copy.12 = f32[8,8,64]{2,1,0:T(8,128)} copy(f32[8,8,64]{2,1,0:T(8,128)S(1)} %get-tuple-element.4) | data formatting | bytes 32768

commit v4 on v3

--- a/solution.py
+++ b/solution.py
@@ -53,14 +53,14 @@
     rhs_hbm, alpha_hbm, bx_hbm, by_hbm, bz_hbm,
     fine_ref, one_ref, bottom_ref,
     raw, ext0, work0, pair0,
-    raw1, packed1, coef1, work1, rhs1, pair1,
-    packed2, coef2, basis,
+    packed1, coef1, work1, rhs1, part1, send1, land1, pair1,
+    packed2, coef2, land2, basis,
     gather_y, gather_x,
     load_sem, out_sem, send_sem, recv_sem, more_send, more_recv, row_send, row_recv, known_x, known_y,
 ):
     gx = lax.axis_index("gx")
     gy = lax.axis_index("gy")
-    n0, n1, n2 = raw.shape[1], raw1.shape[1], raw1.shape[1] // 2
+    n0, n1, n2 = raw.shape[1], raw.shape[1] // 2, raw.shape[1] // 4
 
     for i, src in enumerate((rhs_hbm, alpha_hbm, bx_hbm, by_hbm, bz_hbm)):
         pltpu.make_async_copy(src, raw.at[i], load_sem).start()
@@ -108,40 +108,40 @@
         copy = pltpu.make_async_remote_copy(src, dst, ssem, rsem, device_id=(gx + dx, gy + dy), device_id_type=MESH)
         return copy, has(dx, dy), has(-dx, -dy)
 
-    def exchange(which, ref, own, lead, corner=HALO, skip=()):
+    def exchange(which, part):
+        return [
+            remote(*part(dx, dy), send_sem.at[which, j], recv_sem.at[which, j], dx, dy)
+            for j, (dx, dy) in enumerate(DIRECTIONS)
+        ]
+
+    def exchange_fine(ref, own):
         out = []
-        for j, (dx, dy) in enumerate(DIRECTIONS):
-            if (dx, dy) in skip:
-                continue
-            depth = corner if dx * dy != 0 else HALO
-            (sx, tx), (sy, ty) = spans(dx, own, depth), spans(dy, own, depth)
-            src, dst = (ref.at[:, sx, sy], ref.at[:, tx, ty]) if lead else (ref.at[sx, sy], ref.at[tx, ty])
-            out.append(remote(src, dst, send_sem.at[which, j], recv_sem.at[which, j], dx, dy))
-        return out
-
-    def exchange_fine(ref, own):
-        out = exchange(0, ref, own, True, HALO - 1, ((0, 1), (0, -1)))
-        corners, sides = out[:4], out[4:]
-        more = []
+        deep = HALO - 1
 
         def add(src, dst, dx, dy):
-            k = len(more)
-            more.append(remote(src, dst, more_send.at[k], more_recv.at[k], dx, dy))
+            k = len(out)
+            ssem, rsem = (send_sem.at[0, k], recv_sem.at[0, k]) if k < 8 else (more_send.at[k - 8], more_recv.at[k - 8])
+            out.append(remote(src, dst, ssem, rsem, dx, dy))
 
         for dx, dy in DIRECTIONS[:4]:
+            (sx, tx), (sy, ty) = spans(dx, own, deep - 1), spans(dy, own, deep - 1)
+            add(ref.at[:, sx, sy], ref.at[:, tx, ty], dx, dy)
             if dy == -1:
-                (sx, tx), (sy, ty) = spans(dx, own, 1, HALO - 1), spans(dy, own, 1)
+                (sx, tx), (sy, ty) = spans(dx, own, 1, deep - 1), spans(dy, own, 1)
                 add(ref.at[0, sx, sy], ref.at[0, tx, ty], dx, dy)
             if dx == -1:
-                (sx, tx), (sy, ty) = spans(dx, own, 1), spans(dy, own, 1, HALO - 1)
+                (sx, tx), (sy, ty) = spans(dx, own, 1), spans(dy, own, 1, deep - 1)
                 add(ref.at[3, sx, sy], ref.at[3, tx, ty], dx, dy)
         whole = pl.ds(HALO, own)
         for dy in (1, -1):
-            sy, ty = spans(dy, own)
+            sy, ty = spans(dy, own, deep)
             add(ref.at[pl.ds(0, 3), whole, sy], ref.at[pl.ds(0, 3), whole, ty], 0, dy)
-            sy, ty = spans(dy, own, HALO - 1)
+            sy, ty = spans(dy, own, deep - 1)
             add(ref.at[pl.ds(3, 2), whole, sy], ref.at[pl.ds(3, 2), whole, ty], 0, dy)
-        return corners + more + sides
+        for dx in (1, -1):
+            sx, tx = spans(dx, own, deep)
+            add(ref.at[:, sx, whole], ref.at[:, tx, whole], dx, 0)
+        return out
 
     def start(copies):
         for copy, to, _ in copies:
@@ -168,6 +168,9 @@
         bx_in = jnp.concatenate([bx[:1] * x_inner, bx[1:]], 0)
         return diag, bx_in, by_in, bz_in
 
+    for ref in (part1, land1, land2):
+        ref[...] = jnp.zeros(ref.shape, F32)
+
     pltpu.make_async_copy(raw, raw, load_sem).wait()
 
     own = pl.ds(HALO, n0)
@@ -181,7 +184,7 @@
     tell(0)
 
     def halves(ref, n):
-        return ref[:, pl.ds(0, n, stride=2), :], ref[:, pl.ds(1, n, stride=2), :]
+        return ref[pl.ds(0, n), pl.ds(0, n, stride=2), :], ref[pl.ds(0, n), pl.ds(1, n, stride=2), :]
 
     def coarsen(alpha, bx, by, bz, pairs, width):
         n = bx.shape[0] // 2
@@ -193,10 +196,10 @@
         def zsum(v):
             return v + roll(v, -width, 2)
 
-        pairs[0, :, pl.ds(0, 2 * n)] = zsum(sum(xs(alpha)))
-        pairs[1, :, pl.ds(0, 2 * n)] = zsum(xs(bx)[0])
-        pairs[2, :, pl.ds(0, 2 * n)] = zsum(sum(xs(by)))
-        pairs[3, :, pl.ds(0, 2 * n)] = sum(xs(bz))
+        pairs[0, pl.ds(0, n), pl.ds(0, 2 * n)] = zsum(sum(xs(alpha)))
+        pairs[1, pl.ds(0, n), pl.ds(0, 2 * n)] = zsum(xs(bx)[0])
+        pairs[2, pl.ds(0, n), pl.ds(0, 2 * n)] = zsum(sum(xs(by)))
+        pairs[3, pl.ds(0, n), pl.ds(0, 2 * n)] = sum(xs(bz))
         a0, a1 = halves(pairs.at[0], n)
         x0, x1 = halves(pairs.at[1], n)
         y0, _ = halves(pairs.at[2], n)
@@ -209,17 +212,21 @@
     lane = lane_of(diag.shape)
     packed1[0, own, own, :] = jnp.where(lane % 2 == 0, diag, roll(bx_in, 1, 2))
     packed1[1, own, own, :] = jnp.where(lane % 2 == 0, by_in, roll(bz_in, 1, 2))
-    sent1 = exchange(1, packed1, n1, True)
-    start(sent1)
 
     alpha2, bx2, by2, bz2 = coarsen(alpha1, bx1, by1, bz1, pair1, 2)
     diag, bx_in, by_in, bz_in = own_coefs(alpha2, bx2, by2, bz2, 1.0, 4)
-    own = pl.ds(HALO, n2)
     lane = lane_of(diag.shape) % 4
     mixed = jnp.where(lane < 2, jnp.where(lane == 0, diag, roll(bx_in, 1, 2)), jnp.where(lane == 2, roll(by_in, 2, 2), roll(bz_in, 3, 2)))
-    packed2[own, own, :] = mixed
-    sent2 = exchange(2, packed2, n2, False)
-    start(sent2)
+    for i in range(2):
+        for j in range(2):
+            packed1[2, pl.ds(HALO + n2 * i, n2), pl.ds(HALO + n2 * j, n2), :] = mixed
+
+    def edges(dx, dy):
+        (sx, tx), (sy, ty) = spans(dx, n1), spans(dy, n1)
+        return packed1.at[:, sx, sy], packed1.at[:, tx, ty]
+
+    sent1 = exchange(1, edges)
+    start(sent1)
 
     def border(ref, index, n, value):
         for flag, at in ((gx == 0, 0), (gx == nx - 1, n + HALO)):
@@ -245,23 +252,7 @@
     border(ext0, (2,), n0, ones(1))
     border(packed1, (0,), n1, ones(2))
     border(packed1, (1,), n1, zeros)
-    border(rhs1, (), n1, zeros)
-
-    def border2(ref, value):
-        for flag, at in ((gx == 0, 0), (gx == nx - 1, n2 + HALO)):
-
-            @pl.when(flag)
-            def _(at=at):
-                ref[pl.ds(at, HALO)] = value((HALO,) + ref.shape[1:])
-
-        for flag, at in ((gy == 0, 0), (gy == ny - 1, n2 + HALO)):
-
-            @pl.when(flag)
-            def _(at=at):
-                ref[:, pl.ds(at, HALO)] = value((ref.shape[0], HALO, LANES))
-
-    border2(packed2, ones(4))
-    border2(basis.at[0], zeros)
+    border(packed1, (2,), n1, ones(4))
 
     def whole_diag(part, bx, by, n, scale):
         rows = part.shape[0]
@@ -272,35 +263,33 @@
         bxu = jnp.concatenate([bx[1:rows], jnp.zeros_like(bx[:1])], 0)
         return part + scale * (jnp.where(at_x, bxu, 0.0) + jnp.where(at_y, roll(by, -1, 1), 0.0))
 
-    def sweep(number, faces, work, n, width, finish):
+    def sweep(number, first, rows, faces, work, width, finish, clip=None):
         coefs = steps()
-        first, last = number + 1, n + 2 * HALO - number - 1
-        rows = {22: 2, 20: 4, 18: 6, 16: 4, 14: 7, 12: 6, 10: 5, 8: 4}[last - first]
         source, target = 6 + number % 2, 7 - number % 2
 
         def body(i, carry):
-            at = first + i * rows
-            here = pl.ds(at, rows)
+            at = first + i * rows[1]
+            here = pl.ds(at, rows[1])
             x = work[source, here]
-            total = faces[0][here] * work[source, pl.ds(at - 1, rows)]
-            total = total + faces[0][pl.ds(at + 1, rows)] * work[source, pl.ds(at + 1, rows)]
+            total = faces[0][here] * work[source, pl.ds(at - 1, rows[1])]
+            total = total + faces[0][pl.ds(at + 1, rows[1])] * work[source, pl.ds(at + 1, rows[1])]
             total = total + faces[1][here] * roll(x, 1, 1) + work[2, here] * roll(x, -1, 1)
             total = total + faces[2][here] * roll(x, width, 2) + work[3, here] * roll(x, -width, 2)
-            scaled = work[1, here] - x + work[0, here] * total
             if number == 3:
-                finish(at, rows, work[4, here] * scaled)
+                finish(at, rows[1], work[4, here], work[1, here] - x, work[0, here], total)
             else:
                 a, b = coefs[number]
+                scaled = work[1, here] - x + work[0, here] * total
                 update = a * (x if number == 0 else work[5, here]) + b * scaled
+                x = x + update
+                if clip is not None:
+                    col = lax.broadcasted_iota(jnp.int32, x.shape, 1)
+                    x = jnp.where(jnp.logical_and(col >= HALO, col < HALO + clip), x, 0.0)
                 work[5, here] = update
-                work[target, here] = x + update
+                work[target, here] = x
             return carry
 
-        lax.fori_loop(0, (last - first) // rows, body, 0, unroll=True)
-
-    def smooth(faces, work, n, width, finish):
-        for number in range(4):
-            sweep(number, faces, work, n, width, finish)
+        lax.fori_loop(0, rows[0], body, 0, unroll=True)
 
     def prepare(faces, work, diag, scale, width):
         inverse = 1.0 / diag
@@ -320,26 +309,58 @@
     prepare(faces0, work0, whole_diag(ext0[2], ext0[3], ext0[0], n0, 16.0), 16.0, 1)
     begin(work0, ext0[1], 16.0)
 
-    def halve(pairs, width):
-        def finish(at, rows, resid):
-            summed = resid.reshape((rows // 2, 2) + resid.shape[1:])
+    def halve(pairs, first, width):
+        def finish(at, resid):
+            rows = resid.shape[0] // 2
+            summed = resid.reshape((rows, 2) + resid.shape[1:])
             summed = summed[:, 0] + summed[:, 1]
-            half = lax.div(at - HALO, 2)
-            pairs[pl.ds(half, rows // 2)] = summed + roll(summed, -width, 2)
+            pairs[pl.ds(lax.div(at - first, 2), rows)] = summed + roll(summed, -width, 2)
 
         return finish
 
-    def restrict(pairs, n):
-        even = pairs[:, pl.ds(HALO, n, stride=2), :]
-        odd = pairs[:, pl.ds(HALO + 1, n, stride=2), :]
-        return (even + odd) * 0.125
-
     down0 = pair0.at[4]
-    smooth(faces0, work0, n0, 1, halve(down0, 1))
-    own = pl.ds(HALO, n1)
-    rhs1[own, own, :] = restrict(down0, n1)
-    sent3 = exchange(3, rhs1, n1, False, HALO - 1)
-    start(sent3)
+    keep0 = halve(down0, 2, 1)
+
+    def partial(at, rows, diag, gap, scaled, total):
+        row = at + lax.broadcasted_iota(jnp.int32, gap.shape, 0)
+        col = lax.broadcasted_iota(jnp.int32, gap.shape, 1)
+        in_x = jnp.logical_and(row >= HALO, row < HALO + n0)
+        in_y = jnp.logical_and(col >= HALO, col < HALO + n0)
+        near_y = jnp.logical_and(col >= HALO - 2, col < HALO + n0 + 2)
+        mine = jnp.where(jnp.logical_and(in_x, in_y), diag * gap, 0.0)
+        keep0(at, mine + jnp.where(jnp.logical_or(in_y, jnp.logical_and(in_x, near_y)), 16.0 * total, 0.0))
+
+    sweep(0, 2, (5, 4), faces0, work0, 1, None)
+    sweep(1, 3, (3, 6), faces0, work0, 1, None)
+    sweep(2, 4, (4, 4), faces0, work0, 1, None, n0)
+    for at in (1, HALO + n0):
+        work0[7, pl.ds(at, 3)] = jnp.zeros((3,) + work0.shape[2:], F32)
+    sweep(3, 2, (5, 4), faces0, work0, 1, partial)
+    count = n1 + HALO
+    terms = (down0[:, pl.ds(0, count, stride=2), :] + down0[:, pl.ds(1, count, stride=2), :]) * 0.125
+    part1[pl.ds(HALO - 1, n1 + 2), pl.ds(HALO - 2, count), :] = terms
+    halved = part1[...].reshape(rhs1.shape)
+    even = lane_of(send1.shape) % 2 == 0
+    send1[...] = jnp.where(even, halved[:, 0], roll(halved[:, 1], 1, 2))
+
+    def outer(dx, dy):
+        half = n1 // 2
+        sx, tx = {
+            0: (pl.ds(1, half + 2), pl.ds(1, half + 2)),
+            1: (pl.ds(half, 3), pl.ds(0, 3)),
+            -1: (pl.ds(1, 3), pl.ds(half + 1, 3)),
+        }[dx]
+        wide = HALO + 1
+        sy, ty = {
+            0: (pl.ds(HALO - 1, n1 + 2), pl.ds(HALO - 1, n1 + 2)),
+            1: (pl.ds(n1 + HALO + 1 - wide, wide), pl.ds(HALO + 1 - wide, wide)),
+            -1: (pl.ds(HALO - 1, wide), pl.ds(HALO - 1 + n1, wide)),
+        }[dy]
+        land = land1.at[2 if dx * dy != 0 else 1 if dx != 0 else 0]
+        return send1.at[sx, sy], land.at[tx, ty]
+
+    sent2 = exchange(2, outer)
+    start(sent2)
 
     own = pl.ds(HALO, n0)
     store = pltpu.make_async_copy(work0.at[7, own, own], fine_ref, out_sem)
@@ -354,7 +375,12 @@
     faces1 = (coef1.at[0], coef1.at[1], coef1.at[2])
     prepare(faces1, work1, whole_diag(part, coef1[0], coef1[1], n1, 4.0), 4.0, 2)
 
-    arrive(sent2)
+    outer_at = HALO + n1
+    low, high = pl.ds(0, 2 * HALO), pl.ds(outer_at, HALO)
+    packed2[low, low] = packed1[2, low, low]
+    packed2[low, pl.ds(2 * HALO, HALO)] = packed1[2, low, high]
+    packed2[pl.ds(2 * HALO, HALO), low] = packed1[2, high, low]
+    packed2[pl.ds(2 * HALO, HALO), pl.ds(2 * HALO, HALO)] = packed1[2, high, high]
     mixed = packed2[...] * SHRINK
     bx_in, by_in, bz_in = roll(mixed, -1, 2), roll(mixed, -2, 2), roll(mixed, -3, 2)
     coef2[0] = whole_diag(mixed, bx_in, by_in, n2, 1.0)
@@ -364,16 +390,33 @@
     coef2[4] = bz_in
     coef2[5] = roll(bz_in, -4, 2)
 
-    arrive(sent3)
+    arrive(sent2)
     told(1)
     tell(2)
-    begin(work1, rhs1[...], 4.0)
+    summed = send1[...] + land1[0] + land1[1] + land1[2]
+    rhs1[:, 0] = summed
+    rhs1[:, 1] = roll(summed, -1, 2)
+    begin(work1, rhs1[...].reshape(part1.shape), 4.0)
     down1 = pair1.at[4]
-    smooth(faces1, work1, n1, 2, halve(down1, 2))
-    own = pl.ds(HALO, n2)
-    basis[0, own, own, :] = restrict(down1, n2)
-    sent4 = exchange(4, basis.at[0], n2, False, HALO - 1)
-    start(sent4)
+    keep1 = halve(down1, HALO, 2)
+
+    def whole(at, rows, diag, gap, scaled, total):
+        keep1(at, diag * (gap + scaled * total))
+
+    for number, rows in enumerate(((2, 7), (2, 6), (2, 5), (2, 4))):
+        sweep(number, number + 1, rows, faces1, work1, 2, whole)
+    rhs2 = (down1[:, pl.ds(HALO, n2, stride=2), :] + down1[:, pl.ds(HALO + 1, n2, stride=2), :]) * 0.125
+    lane = lane_of(rhs2.shape[1:]) % 4
+    mixed = rhs2[0]
+    for i in range(1, n2):
+        mixed = jnp.where(lane == i, roll(rhs2[i], i, 1), mixed)
+    land2[1, pl.ds(HALO, n2), :] = mixed
+
+    def block(dx, dy):
+        return land2.at[1, pl.ds(HALO, n2)], land2.at[1 - dx, pl.ds(HALO - n2 * dy, n2)]
+
+    sent3 = exchange(3, block)
+    start(sent3)
 
     def compacted(value, width):
         rows = value.reshape((-1, LANES))
@@ -385,9 +428,12 @@
     own = pl.ds(HALO, n1)
     one_ref[...] = compacted(work1[7, own, own, :], 2)
 
-    arrive(sent4)
+    arrive(sent3)
     told(2)
     tell(3)
+    for i in range(3):
+        for j in range(n2):
+            basis[0, n2 * i + j] = land2[i] if j == 0 else roll(land2[i], -j, 1)
     for number in range(4):
         first, last = number + 1, n2 + 2 * HALO - number - 1
         here = pl.ds(first, last - first)
@@ -469,7 +515,7 @@
             total = term if total is None else total + term
     bottom_ref[...] = compacted(total, 4)[:, HALO:, :]
 
-    for copies in (sent0, sent1, sent2, sent3, sent4):
+    for copies in (sent0, sent1, sent2, sent3):
         leave(copies)
     for copy in (sent5, sent6, store):
         copy.wait()
@@ -499,24 +545,27 @@
             pltpu.VMEM((5, n0, n0, nz), F32),
             pltpu.VMEM((5, e0, e0, nz), F32),
             pltpu.VMEM((8, e0, e0, nz), F32),
-            pltpu.VMEM((5, n1, e0, nz), F32),
-            pltpu.VMEM((4, n1, n1, nz), F32),
-            pltpu.VMEM((2, e1, e1, nz), F32),
+            pltpu.VMEM((5, n1 + 2, e0, nz), F32),
+            pltpu.VMEM((3, e1, e1, nz), F32),
             pltpu.VMEM((3, e1, e1, nz), F32),
             pltpu.VMEM((8, e1, e1, nz), F32),
+            pltpu.VMEM((e1 // 2, 2, e1, nz), F32),
             pltpu.VMEM((e1, e1, nz), F32),
+            pltpu.VMEM((e1 // 2, e1, nz), F32),
+            pltpu.VMEM((3, e1 // 2, e1, nz), F32),
             pltpu.VMEM((5, n2, e1, nz), F32),
             pltpu.VMEM((e2, 16, nz), F32),
             pltpu.VMEM((6, e2, 16, nz), F32),
+            pltpu.VMEM((3, 16, nz), F32),
             pltpu.VMEM((5, e2, 16, nz), F32),
             pltpu.VMEM((ny, 1, nz), F32),
             pltpu.VMEM((nx, 1, nz), F32),
             pltpu.SemaphoreType.DMA,
             pltpu.SemaphoreType.DMA,
-            pltpu.SemaphoreType.DMA((5, 8)),
-            pltpu.SemaphoreType.DMA((5, 8)),
-            pltpu.SemaphoreType.DMA((8,)),
-            pltpu.SemaphoreType.DMA((8,)),
+            pltpu.SemaphoreType.DMA((4, 8)),
+            pltpu.SemaphoreType.DMA((4, 8)),
+            pltpu.SemaphoreType.DMA((6,)),
+            pltpu.SemaphoreType.DMA((6,)),
             pltpu.SemaphoreType.DMA((2,)),
             pltpu.SemaphoreType.DMA((2,)),
             pltpu.SemaphoreType.REGULAR((4,)),

time: 49 us -> 47.2 us (0.963)
  Pallas kernels: 46.3 us -> 44.5 us
    pallas_call x1, Pallas kernels: 46.3 us -> 44.5 us  [per_device(): pl.pallas_call(body, out_shape=(pltpu.VMEM((n0, n0, nz), F32), pltpu.VMEM...]
where the time goes in v4:
time: 47.2 us; the launch traced here: 47 us
  Pallas kernels  44.5 us (94%)
  local copies, waits for them, and re-layouts  1.87 us (4%)
  between operations  0.64 us (1%)
    pallas_call x1, Pallas kernels, per_device(): pl.pallas_call(body, out_shape=(pltpu.VMEM((n0, n0, nz), F32), pltpu.VMEM...  44.5 us
    unnamed x3, local copies, waits for them, and re-layouts  1.87 us

profile of v4, /device:TPU:1, one launch (start us, length us, event | category | flops | bytes accessed | tf_op | source)
XLA Modules:
  0.0 47.0 jit_solution(5294664664689607148)
XLA Ops:
  0.6 44.5 %vcycle_down.1 = (f32[16,16,128]{2,1,0:T(8,128)S(1)}, f32[8,8,64]{2,1,0:T(8,128)S(1)}, f32[4,4,32]{2,1,0:T(4,128)S(1)}) custom-call(f32[16,16,128]{2,1,0:T(8,128)} %refs_0_.1, f32[16,16,128]{2,1,0:T(8,128)} %refs_1_.1, f32[16,16,128]{2,1,0:T(8,128)} %refs_2_.1, f32[16,16,128]{2,1,0:T(8,128)} %refs_3_.1, f32[16,16,128]{2,1,0:T(8,128)} %refs_4_.1), custom_call_target="tpu_custom_call" | custom-call | flops 40000000 | bytes 800000 | tf_op jit(solution)/shard_map/vcycle_down/pallas_call | solution.py:535
  45.2 0.7 %copy.11 = f32[16,16,128]{2,1,0:T(8,128)} copy(f32[16,16,128]{2,1,0:T(8,128)S(1)} %get-tuple-element.3) | data formatting | bytes 262144
  45.8 0.6 %copy.13 = f32[4,4,32]{2,1,0:T(4,128)} copy(f32[4,4,32]{2,1,0:T(4,128)S(1)} %get-tuple-element.5) | data formatting | bytes 4096
  46.4 0.6 %copy.12 = f32[8,8,64]{2,1,0:T(8,128)} copy(f32[8,8,64]{2,1,0:T(8,128)S(1)} %get-tuple-element.4) | data formatting | bytes 32768

commit v5 on v4

--- a/solution.py
+++ b/solution.py
@@ -54,9 +54,9 @@
     fine_ref, one_ref, bottom_ref,
     raw, ext0, work0, pair0,
     packed1, coef1, work1, rhs1, part1, send1, land1, pair1,
-    packed2, coef2, land2, basis,
-    gather_y, gather_x,
-    load_sem, out_sem, send_sem, recv_sem, more_send, more_recv, row_send, row_recv, known_x, known_y,
+    coef_blocks, coef_cols, coef2, rhs_blocks, rhs_cols, basis,
+    gather_x,
+    load_sem, out_sem, send_sem, recv_sem, more_send, more_recv, line_send, line_recv, row_send, row_recv, known_x, known_y,
 ):
     gx = lax.axis_index("gx")
     gy = lax.axis_index("gy")
@@ -93,16 +93,16 @@
         pl.semaphore_signal(barrier, inc=1, device_id=peer_x(o), device_id_type=MESH)
         pl.semaphore_signal(barrier, inc=1, device_id=peer_y(o), device_id_type=MESH)
 
-    def tell(number):
-        for sems, peer, count in ((known_x, peer_x, nx), (known_y, peer_y, ny)):
-            if 2**number < count // 2:
-                for o in (2**number, -(2**number)):
-                    pl.semaphore_signal(sems.at[number], inc=1, device_id=peer(o), device_id_type=MESH)
-
-    def told(number):
-        for sems, count in ((known_x, nx), (known_y, ny)):
-            if 2**number < count // 2:
-                pl.semaphore_wait(sems.at[number], 2)
+    def tell(number, sems, peer, count):
+        if 2**number < count // 2:
+            for o in (2**number, -(2**number)):
+                pl.semaphore_signal(sems.at[number], inc=1, device_id=peer(o), device_id_type=MESH)
+
+    def told(number, sems, peer, count):
+        if 2**number < count // 2:
+            pl.semaphore_wait(sems.at[number], 2)
+
+    along_x, along_y = (known_x, peer_x, nx), (known_y, peer_y, ny)
 
     def remote(src, dst, ssem, rsem, dx, dy):
         copy = pltpu.make_async_remote_copy(src, dst, ssem, rsem, device_id=(gx + dx, gy + dy), device_id_type=MESH)
@@ -168,7 +168,7 @@
         bx_in = jnp.concatenate([bx[:1] * x_inner, bx[1:]], 0)
         return diag, bx_in, by_in, bz_in
 
-    for ref in (part1, land1, land2):
+    for ref in (part1, land1):
         ref[...] = jnp.zeros(ref.shape, F32)
 
     pltpu.make_async_copy(raw, raw, load_sem).wait()
@@ -181,7 +181,8 @@
     pl.semaphore_wait(barrier, greeted)
     sent0 = exchange_fine(ext0, n0)
     start(sent0)
-    tell(0)
+    tell(0, *along_x)
+    tell(0, *along_y)
 
     def halves(ref, n):
         return ref[pl.ds(0, n), pl.ds(0, n, stride=2), :], ref[pl.ds(0, n), pl.ds(1, n, stride=2), :]
@@ -217,9 +218,8 @@
     diag, bx_in, by_in, bz_in = own_coefs(alpha2, bx2, by2, bz2, 1.0, 4)
     lane = lane_of(diag.shape) % 4
     mixed = jnp.where(lane < 2, jnp.where(lane == 0, diag, roll(bx_in, 1, 2)), jnp.where(lane == 2, roll(by_in, 2, 2), roll(bz_in, 3, 2)))
-    for i in range(2):
-        for j in range(2):
-            packed1[2, pl.ds(HALO + n2 * i, n2), pl.ds(HALO + n2 * j, n2), :] = mixed
+    first4 = pl.ds(0, n2)
+    coef_blocks[1, gy, :, first4] = mixed
 
     def edges(dx, dy):
         (sx, tx), (sy, ty) = spans(dx, n1), spans(dy, n1)
@@ -252,7 +252,22 @@
     border(ext0, (2,), n0, ones(1))
     border(packed1, (0,), n1, ones(2))
     border(packed1, (1,), n1, zeros)
-    border(packed1, (2,), n1, ones(4))
+    for flag, at in ((gx == 0, 0), (gx == nx - 1, 2)):
+
+        @pl.when(flag)
+        def _(at=at):
+            coef_blocks[at] = zeros(coef_blocks.shape[1:])
+            rhs_blocks[at] = zeros(rhs_blocks.shape[1:])
+
+    wide = n2 * (ny // 4)
+    line, head, tail = pl.ds(HALO, wide), pl.ds(0, HALO), pl.ds(HALO + wide, HALO)
+    for ref in (coef_cols, rhs_cols):
+        for part in (head, tail):
+            at = (slice(None),) * (len(ref.shape) - 2) + (part,)
+            ref[at] = zeros(ref.shape[:-2] + (HALO, LANES))
+
+    told(0, *along_y)
+    tell(1, *along_y)
 
     def whole_diag(part, bx, by, n, scale):
         rows = part.shape[0]
@@ -303,8 +318,10 @@
         work[6] = work[1] * (1.0 / THETA)
 
     arrive(sent0)
-    told(0)
-    tell(1)
+    told(0, *along_x)
+    tell(1, *along_x)
+    told(1, *along_y)
+    tell(2, *along_y)
     faces0 = (ext0.at[3], ext0.at[0], ext0.at[4])
     prepare(faces0, work0, whole_diag(ext0[2], ext0[3], ext0[0], n0, 16.0), 16.0, 1)
     begin(work0, ext0[1], 16.0)
@@ -362,6 +379,13 @@
     sent2 = exchange(2, outer)
     start(sent2)
 
+    told(2, *along_y)
+    mine = coef_blocks.at[1, gy, :, first4]
+    for o in range(1, ny):
+        pltpu.make_async_remote_copy(
+            mine, mine, line_send.at[0], line_recv.at[0], device_id=peer_y(o), device_id_type=MESH
+        ).start()
+
     own = pl.ds(HALO, n0)
     store = pltpu.make_async_copy(work0.at[7, own, own], fine_ref, out_sem)
     store.start()
@@ -375,24 +399,9 @@
     faces1 = (coef1.at[0], coef1.at[1], coef1.at[2])
     prepare(faces1, work1, whole_diag(part, coef1[0], coef1[1], n1, 4.0), 4.0, 2)
 
-    outer_at = HALO + n1
-    low, high = pl.ds(0, 2 * HALO), pl.ds(outer_at, HALO)
-    packed2[low, low] = packed1[2, low, low]
-    packed2[low, pl.ds(2 * HALO, HALO)] = packed1[2, low, high]
-    packed2[pl.ds(2 * HALO, HALO), low] = packed1[2, high, low]
-    packed2[pl.ds(2 * HALO, HALO), pl.ds(2 * HALO, HALO)] = packed1[2, high, high]
-    mixed = packed2[...] * SHRINK
-    bx_in, by_in, bz_in = roll(mixed, -1, 2), roll(mixed, -2, 2), roll(mixed, -3, 2)
-    coef2[0] = whole_diag(mixed, bx_in, by_in, n2, 1.0)
-    coef2[1] = bx_in
-    coef2[2] = by_in
-    coef2[3] = roll(by_in, -1, 1)
-    coef2[4] = bz_in
-    coef2[5] = roll(bz_in, -4, 2)
-
     arrive(sent2)
-    told(1)
-    tell(2)
+    told(1, *along_x)
+    tell(2, *along_x)
     summed = send1[...] + land1[0] + land1[1] + land1[2]
     rhs1[:, 0] = summed
     rhs1[:, 1] = roll(summed, -1, 2)
@@ -410,30 +419,95 @@
     mixed = rhs2[0]
     for i in range(1, n2):
         mixed = jnp.where(lane == i, roll(rhs2[i], i, 1), mixed)
-    land2[1, pl.ds(HALO, n2), :] = mixed
-
-    def block(dx, dy):
-        return land2.at[1, pl.ds(HALO, n2)], land2.at[1 - dx, pl.ds(HALO - n2 * dy, n2)]
-
-    sent3 = exchange(3, block)
-    start(sent3)
-
-    def compacted(value, width):
+    rhs_blocks[1, gy, first4] = mixed
+
+    mine = rhs_blocks.at[1, gy, first4]
+    for dx in (1, -1, 0):
+
+        def spread(dx=dx):
+            for o in sorted(range(1 if dx == 0 else 0, ny), key=lambda o: -min(o, ny - o)):
+                pltpu.make_async_remote_copy(
+                    mine, rhs_blocks.at[1 - dx, gy, first4], line_send.at[3 + dx], line_recv.at[3 + dx],
+                    device_id=(gx + dx, lax.rem(gy + o, ny)), device_id_type=MESH,
+                ).start()
+
+        if dx == 0:
+            spread()
+        else:
+            pl.when(has(dx, 0))(spread)
+
+    told(2, *along_x)
+    tell(3, *along_x)
+
+    def bytes_of(ref, sem):
+        return pltpu.make_async_copy(ref, ref, sem)
+
+    others = pl.ds(0, ny - 1)
+    bytes_of(coef_blocks.at[1, others, :, first4], line_recv.at[0]).wait()
+    passed = []
+    for dx in (1, -1):
+        src, dst = coef_blocks.at[1, :, :, first4], coef_blocks.at[1 - dx, :, :, first4]
+        passed.append(remote(src, dst, line_send.at[(dx + 1) // 2 * 4 + 1], line_recv.at[(dx + 1) // 2 * 4 + 1], dx, 0))
+    start(passed)
+
+    def compacted(value, width, shift=0):
         rows = value.reshape((-1, LANES))
         count = LANES // width
-        pick = lax.broadcasted_iota(jnp.int32, (LANES, count), 0) == width * lax.broadcasted_iota(jnp.int32, (LANES, count), 1)
+        pick = lax.broadcasted_iota(jnp.int32, (LANES, count), 0) == shift + width * lax.broadcasted_iota(jnp.int32, (LANES, count), 1)
         out = jnp.dot(rows, pick.astype(F32), precision=lax.Precision.HIGHEST, preferred_element_type=F32)
         return out.reshape(value.shape[:-1] + (count,))
 
     own = pl.ds(HALO, n1)
     one_ref[...] = compacted(work1[7, own, own, :], 2)
 
-    arrive(sent3)
-    told(2)
-    tell(3)
-    for i in range(3):
-        for j in range(n2):
-            basis[0, n2 * i + j] = land2[i] if j == 0 else roll(land2[i], -j, 1)
+    residue = lane_of(basis.shape[2:]) % 4
+
+    def grouped(blocks, shift):
+        out = None
+        for q in range(4):
+            moved = roll(blocks[q], q - shift, 1) if q != shift else blocks[q]
+            out = moved if out is None else jnp.where(residue == q, moved, out)
+        return out
+
+    def joined(ref):
+        side = lane_of((ref.shape[0], HALO, LANES)) % 4
+        ref[:, head] = jnp.where(side != 0, roll(ref[:, pl.ds(wide, HALO)], 1, 2), 0.0)
+        ref[:, tail] = jnp.where(side != 3, roll(ref[:, pl.ds(HALO, HALO)], -1, 2), 0.0)
+
+    arrive(passed)
+    for s in range(3):
+        for b in range(ny):
+            q, p = divmod(b, ny // 4)
+            for i in range(n2):
+                coef_cols[s, i, q, pl.ds(HALO + n2 * p, n2)] = coef_blocks[s, b, i, first4]
+    for s in range(3):
+        for i in range(n2):
+            blocks = [coef_cols[s, i, q] * SHRINK for q in range(4)]
+            for a, at in enumerate((0, 1, 2, 4)):
+                coef2[at, n2 * s + i] = grouped(blocks, a)
+    for at in (0, 1, 2, 4):
+        joined(coef2.at[at])
+    diag, bx_in, by_in = coef2[0], coef2[1], coef2[2]
+    row = lax.broadcasted_iota(jnp.int32, diag.shape, 0)
+    col = lax.broadcasted_iota(jnp.int32, diag.shape, 1)
+    bxu = jnp.concatenate([bx_in[1:], jnp.zeros_like(bx_in[:1])], 0)
+    byu = roll(by_in, -1, 1)
+    coef2[0] = diag + jnp.where(row % n2 == n2 - 1, bxu, 0.0) + jnp.where(col % n2 == n2 - 1, byu, 0.0)
+    coef2[3] = byu
+    coef2[5] = roll(coef2[4], -4, 2)
+
+    bytes_of(rhs_blocks.at[1, others, first4], line_recv.at[3]).wait()
+    for dx in (1, -1):
+        arriving = bytes_of(rhs_blocks.at[1 - dx, :, first4], line_recv.at[3 + dx])
+        pl.when(has(-dx, 0))(arriving.wait)
+    for s in range(3):
+        for b in range(ny):
+            q, p = divmod(b, ny // 4)
+            rhs_cols[s, q, pl.ds(HALO + n2 * p, n2)] = rhs_blocks[s, b, first4]
+        blocks = [rhs_cols[s, q] for q in range(4)]
+        for i in range(n2):
+            basis[0, n2 * s + i] = grouped(blocks, i)
+    joined(basis.at[0])
     for number in range(4):
         first, last = number + 1, n2 + 2 * HALO - number - 1
         here = pl.ds(first, last - first)
@@ -445,13 +519,11 @@
         basis[number + 1, here] = coef2[0, here] * x - total
 
     own = pl.ds(HALO, n2)
-    vectors = [basis[i, own, own, :] for i in range(5)]
-    valid = lane_of((n2, LANES)) % 4 == 0
+    vectors = [basis[i, own, line, :] for i in range(5)]
     lane = lane_of((1, LANES))
     row = jnp.zeros((1, LANES), F32)
     for k in range(9):
         product = jnp.sum(vectors[k // 2] * vectors[(k + 1) // 2], axis=0)
-        product = jnp.where(valid, product, 0.0)
         moment = jnp.sum(jnp.sum(product, axis=0, keepdims=True), axis=1, keepdims=True)
         row = jnp.where(lane == k, moment, row)
 
@@ -466,9 +538,8 @@
         pltpu.make_async_copy(others, others, row_recv.at[k]).wait()
         return jnp.sum(slots[...], axis=0), pltpu.make_async_copy(others, others, row_send.at[k])
 
-    row, sent5 = all_sum(row, gather_y, 0, peer_y)
-    told(3)
-    row, sent6 = all_sum(row, gather_x, 1, peer_x)
+    told(3, *along_x)
+    row, sent5 = all_sum(row, gather_x, 0, peer_x)
     moments = [jnp.sum(jnp.where(lane == k, row, 0.0), axis=1, keepdims=True) for k in range(9)]
 
     def inner(u, w):
@@ -511,14 +582,21 @@
     total = None
     for i, c in enumerate(solved):
         if c is not None:
-            term = c * basis[i, pl.ds(HALO, n2), pl.ds(0, 2 * HALO), :]
+            term = c * vectors[i]
             total = term if total is None else total + term
-    bottom_ref[...] = compacted(total, 4)[:, HALO:, :]
-
-    for copies in (sent0, sent1, sent2, sent3):
+    group, place = lax.div(gy, ny // 4), lax.rem(gy, ny // 4)
+    mine = compacted(total, 4, group)
+    bottom = mine[:, :n2]
+    for p in range(1, ny // 4):
+        bottom = jnp.where(place == p, mine[:, n2 * p : n2 * (p + 1)], bottom)
+    bottom_ref[...] = bottom
+
+    for copies in (sent0, sent1, sent2, passed):
         leave(copies)
-    for copy in (sent5, sent6, store):
+    for copy in (sent5, store, bytes_of(coef_blocks.at[1, others, :, first4], line_send.at[0]), bytes_of(rhs_blocks.at[1, others, first4], line_send.at[3])):
         copy.wait()
+    for dx in (1, -1):
+        pl.when(has(dx, 0))(bytes_of(rhs_blocks.at[1, :, first4], line_send.at[3 + dx]).wait)
 
 
 def per_device(right_side, alpha_cells, beta_x, beta_y, beta_z):
@@ -546,7 +624,7 @@
             pltpu.VMEM((5, e0, e0, nz), F32),
             pltpu.VMEM((8, e0, e0, nz), F32),
             pltpu.VMEM((5, n1 + 2, e0, nz), F32),
-            pltpu.VMEM((3, e1, e1, nz), F32),
+            pltpu.VMEM((2, e1, e1, nz), F32),
             pltpu.VMEM((3, e1, e1, nz), F32),
             pltpu.VMEM((8, e1, e1, nz), F32),
             pltpu.VMEM((e1 // 2, 2, e1, nz), F32),
@@ -554,20 +632,23 @@
             pltpu.VMEM((e1 // 2, e1, nz), F32),
             pltpu.VMEM((3, e1 // 2, e1, nz), F32),
             pltpu.VMEM((5, n2, e1, nz), F32),
-            pltpu.VMEM((e2, 16, nz), F32),
-            pltpu.VMEM((6, e2, 16, nz), F32),
-            pltpu.VMEM((3, 16, nz), F32),
-            pltpu.VMEM((5, e2, 16, nz), F32),
-            pltpu.VMEM((ny, 1, nz), F32),
+            pltpu.VMEM((3, ny, n2, 8, nz), F32),
+            pltpu.VMEM((3, n2, 4, 24, nz), F32),
+            pltpu.VMEM((6, e2, 24, nz), F32),
+            pltpu.VMEM((3, ny, 8, nz), F32),
+            pltpu.VMEM((3, 4, 24, nz), F32),
+            pltpu.VMEM((5, e2, 24, nz), F32),
             pltpu.VMEM((nx, 1, nz), F32),
             pltpu.SemaphoreType.DMA,
             pltpu.SemaphoreType.DMA,
-            pltpu.SemaphoreType.DMA((4, 8)),
-            pltpu.SemaphoreType.DMA((4, 8)),
+            pltpu.SemaphoreType.DMA((3, 8)),
+            pltpu.SemaphoreType.DMA((3, 8)),
             pltpu.SemaphoreType.DMA((6,)),
             pltpu.SemaphoreType.DMA((6,)),
-            pltpu.SemaphoreType.DMA((2,)),
-            pltpu.SemaphoreType.DMA((2,)),
+            pltpu.SemaphoreType.DMA((6,)),
+            pltpu.SemaphoreType.DMA((6,)),
+            pltpu.SemaphoreType.DMA((1,)),
+            pltpu.SemaphoreType.DMA((1,)),
             pltpu.SemaphoreType.REGULAR((4,)),
             pltpu.SemaphoreType.REGULAR((4,)),
         ],

time: 47.2 us -> 43.5 us (0.922)
  Pallas kernels: 44.5 us -> 40.8 us
    pallas_call x1, Pallas kernels: 44.5 us -> 40.8 us  [per_device(): pl.pallas_call(body, out_shape=(pltpu.VMEM((n0, n0, nz), F32), pltpu.VMEM...]
where the time goes in v5:
time: 43.5 us; the launch traced here: 43.3 us
  Pallas kernels  40.8 us (94%)
  local copies, waits for them, and re-layouts  1.87 us (4%)
  between operations  0.64 us (1%)
    pallas_call x1, Pallas kernels, per_device(): pl.pallas_call(body, out_shape=(pltpu.VMEM((n0, n0, nz), F32), pltpu.VMEM...  40.8 us
    unnamed x3, local copies, waits for them, and re-layouts  1.87 us

profile of v5, /device:TPU:1, one launch (start us, length us, event | category | flops | bytes accessed | tf_op | source)
XLA Modules:
  0.0 43.3 jit_solution(12910628570422647111)
XLA Ops:
  0.6 40.8 %vcycle_down.1 = (f32[16,16,128]{2,1,0:T(8,128)S(1)}, f32[8,8,64]{2,1,0:T(8,128)S(1)}, f32[4,4,32]{2,1,0:T(4,128)S(1)}) custom-call(f32[16,16,128]{2,1,0:T(8,128)} %refs_0_.1, f32[16,16,128]{2,1,0:T(8,128)} %refs_1_.1, f32[16,16,128]{2,1,0:T(8,128)} %refs_2_.1, f32[16,16,128]{2,1,0:T(8,128)} %refs_3_.1, f32[16,16,128]{2,1,0:T(8,128)} %refs_4_.1), custom_call_target="tpu_custom_call" | custom-call | flops 40000000 | bytes 800000 | tf_op jit(solution)/shard_map/vcycle_down/pallas_call | solution.py:613
  41.4 0.7 %copy.11 = f32[16,16,128]{2,1,0:T(8,128)} copy(f32[16,16,128]{2,1,0:T(8,128)S(1)} %get-tuple-element.3) | data formatting | bytes 262144
  42.1 0.6 %copy.13 = f32[4,4,32]{2,1,0:T(4,128)} copy(f32[4,4,32]{2,1,0:T(4,128)S(1)} %get-tuple-element.5) | data formatting | bytes 4096
  42.7 0.6 %copy.12 = f32[8,8,64]{2,1,0:T(8,128)} copy(f32[8,8,64]{2,1,0:T(8,128)S(1)} %get-tuple-element.4) | data formatting | bytes 32768

commit v6 on v5

--- a/solution.py
+++ b/solution.py
@@ -55,8 +55,8 @@
     raw, ext0, work0, pair0,
     packed1, coef1, work1, rhs1, part1, send1, land1, pair1,
     coef_blocks, coef_cols, coef2, rhs_blocks, rhs_cols, basis,
-    gather_x,
-    load_sem, out_sem, send_sem, recv_sem, more_send, more_recv, line_send, line_recv, row_send, row_recv, known_x, known_y,
+    gather_x, tally,
+    load_sem, out_sem, send_sem, recv_sem, line_send, line_recv, row_send, row_recv, known_x, known_y,
 ):
     gx = lax.axis_index("gx")
     gy = lax.axis_index("gy")
@@ -106,22 +106,20 @@
 
     def remote(src, dst, ssem, rsem, dx, dy):
         copy = pltpu.make_async_remote_copy(src, dst, ssem, rsem, device_id=(gx + dx, gy + dy), device_id_type=MESH)
-        return copy, has(dx, dy), has(-dx, -dy)
+        rows = 1
+        for extent in dst.shape[:-1]:
+            rows *= extent
+        return copy, dx, dy, rows
 
     def exchange(which, part):
-        return [
-            remote(*part(dx, dy), send_sem.at[which, j], recv_sem.at[which, j], dx, dy)
-            for j, (dx, dy) in enumerate(DIRECTIONS)
-        ]
+        return [remote(*part(dx, dy), send_sem.at[which], recv_sem.at[which], dx, dy) for dx, dy in DIRECTIONS]
 
     def exchange_fine(ref, own):
         out = []
         deep = HALO - 1
 
         def add(src, dst, dx, dy):
-            k = len(out)
-            ssem, rsem = (send_sem.at[0, k], recv_sem.at[0, k]) if k < 8 else (more_send.at[k - 8], more_recv.at[k - 8])
-            out.append(remote(src, dst, ssem, rsem, dx, dy))
+            out.append(remote(src, dst, send_sem.at[0], recv_sem.at[0], dx, dy))
 
         for dx, dy in DIRECTIONS[:4]:
             (sx, tx), (sy, ty) = spans(dx, own, deep - 1), spans(dy, own, deep - 1)
@@ -144,16 +142,36 @@
         return out
 
     def start(copies):
-        for copy, to, _ in copies:
-            pl.when(to)(copy.start)
-
-    def arrive(copies):
-        for copy, _, of in copies:
-            pl.when(of)(copy.wait_recv)
-
-    def leave(copies):
-        for copy, to, _ in copies:
-            pl.when(to)(copy.wait_send)
+        for copy, dx, dy, _ in copies:
+            pl.when(has(dx, dy))(copy.start)
+
+    def bytes_of(ref, sem):
+        return pltpu.make_async_copy(ref, ref, sem)
+
+    def settle(copies, sem, way):
+        def waits(ex, ey):
+            rows = sum(r for _, dx, dy, r in copies if (ex == 0 or way * dx != ex) and (ey == 0 or way * dy != ey))
+            bytes_of(tally.at[pl.ds(0, rows)], sem).wait()
+
+        def where(at, count):
+            return {-1: at == 0, 0: jnp.logical_and(at > 0, at < count - 1), 1: at == count - 1}
+
+        at_x, at_y = where(gx, nx), where(gy, ny)
+        inside = jnp.logical_and(at_x[0], at_y[0])
+        pl.when(inside)(lambda: waits(0, 0))
+
+        @pl.when(jnp.logical_not(inside))
+        def _():
+            for ex in (-1, 0, 1):
+                for ey in (-1, 0, 1):
+                    if (ex, ey) != (0, 0):
+                        pl.when(jnp.logical_and(at_x[ex], at_y[ey]))(lambda ex=ex, ey=ey: waits(ex, ey))
+
+    def arrive(copies, which):
+        settle(copies, recv_sem.at[which], -1)
+
+    def leave(copies, which):
+        settle(copies, send_sem.at[which], 1)
 
     x_inner = jnp.where(gx > 0, 1.0, 0.0).astype(F32)
 
@@ -317,7 +335,7 @@
         work[1] = work[0] * rhs * (1.0 / scale)
         work[6] = work[1] * (1.0 / THETA)
 
-    arrive(sent0)
+    arrive(sent0, 0)
     told(0, *along_x)
     tell(1, *along_x)
     told(1, *along_y)
@@ -390,7 +408,7 @@
     store = pltpu.make_async_copy(work0.at[7, own, own], fine_ref, out_sem)
     store.start()
 
-    arrive(sent1)
+    arrive(sent1, 1)
     even = lane_of(packed1.shape[1:]) % 2 == 0
     part = jnp.where(even, packed1[0], 1.0)
     coef1[0] = roll(packed1[0], -1, 2)
@@ -399,7 +417,7 @@
     faces1 = (coef1.at[0], coef1.at[1], coef1.at[2])
     prepare(faces1, work1, whole_diag(part, coef1[0], coef1[1], n1, 4.0), 4.0, 2)
 
-    arrive(sent2)
+    arrive(sent2, 2)
     told(1, *along_x)
     tell(2, *along_x)
     summed = send1[...] + land1[0] + land1[1] + land1[2]
@@ -439,9 +457,6 @@
     told(2, *along_x)
     tell(3, *along_x)
 
-    def bytes_of(ref, sem):
-        return pltpu.make_async_copy(ref, ref, sem)
-
     others = pl.ds(0, ny - 1)
     bytes_of(coef_blocks.at[1, others, :, first4], line_recv.at[0]).wait()
     passed = []
@@ -474,7 +489,8 @@
         ref[:, head] = jnp.where(side != 0, roll(ref[:, pl.ds(wide, HALO)], 1, 2), 0.0)
         ref[:, tail] = jnp.where(side != 3, roll(ref[:, pl.ds(HALO, HALO)], -1, 2), 0.0)
 
-    arrive(passed)
+    for copy, dx, _, _ in passed:
+        pl.when(has(-dx, 0))(copy.wait_recv)
     for s in range(3):
         for b in range(ny):
             q, p = divmod(b, ny // 4)
@@ -497,10 +513,10 @@
     coef2[5] = roll(coef2[4], -4, 2)
 
     bytes_of(rhs_blocks.at[1, others, first4], line_recv.at[3]).wait()
-    for dx in (1, -1):
-        arriving = bytes_of(rhs_blocks.at[1 - dx, :, first4], line_recv.at[3 + dx])
-        pl.when(has(-dx, 0))(arriving.wait)
-    for s in range(3):
+    for s in (1, 0, 2):
+        if s != 1:
+            arriving = bytes_of(rhs_blocks.at[s, :, first4], line_recv.at[4 - s])
+            pl.when(has(s - 1, 0))(arriving.wait)
         for b in range(ny):
             q, p = divmod(b, ny // 4)
             rhs_cols[s, q, pl.ds(HALO + n2 * p, n2)] = rhs_blocks[s, b, first4]
@@ -534,9 +550,21 @@
             pltpu.make_async_remote_copy(
                 slots.at[0], slots.at[o], row_send.at[k], row_recv.at[k], device_id=peer(o), device_id_type=MESH
             ).start()
+        meanwhile()
         others = slots.at[pl.ds(1, count)]
-        pltpu.make_async_copy(others, others, row_recv.at[k]).wait()
-        return jnp.sum(slots[...], axis=0), pltpu.make_async_copy(others, others, row_send.at[k])
+        bytes_of(others, row_recv.at[k]).wait()
+        return jnp.sum(slots[...], axis=0), bytes_of(others, row_send.at[k])
+
+    def meanwhile():
+        for which, copies in enumerate((sent0, sent1, sent2)):
+            leave(copies, which)
+        for copy, dx, _, _ in passed:
+            pl.when(has(dx, 0))(copy.wait_send)
+        for dx in (1, -1):
+            pl.when(has(dx, 0))(bytes_of(rhs_blocks.at[1, :, first4], line_send.at[3 + dx]).wait)
+        bytes_of(rhs_blocks.at[1, others, first4], line_send.at[3]).wait()
+        bytes_of(coef_blocks.at[1, others, :, first4], line_send.at[0]).wait()
+        store.wait()
 
     told(3, *along_x)
     row, sent5 = all_sum(row, gather_x, 0, peer_x)
@@ -590,13 +618,7 @@
     for p in range(1, ny // 4):
         bottom = jnp.where(place == p, mine[:, n2 * p : n2 * (p + 1)], bottom)
     bottom_ref[...] = bottom
-
-    for copies in (sent0, sent1, sent2, passed):
-        leave(copies)
-    for copy in (sent5, store, bytes_of(coef_blocks.at[1, others, :, first4], line_send.at[0]), bytes_of(rhs_blocks.at[1, others, first4], line_send.at[3])):
-        copy.wait()
-    for dx in (1, -1):
-        pl.when(has(dx, 0))(bytes_of(rhs_blocks.at[1, :, first4], line_send.at[3 + dx]).wait)
+    sent5.wait()
 
 
 def per_device(right_side, alpha_cells, beta_x, beta_y, beta_z):
@@ -639,12 +661,11 @@
             pltpu.VMEM((3, 4, 24, nz), F32),
             pltpu.VMEM((5, e2, 24, nz), F32),
             pltpu.VMEM((nx, 1, nz), F32),
+            pltpu.VMEM((1024, nz), F32),
             pltpu.SemaphoreType.DMA,
             pltpu.SemaphoreType.DMA,
-            pltpu.SemaphoreType.DMA((3, 8)),
-            pltpu.SemaphoreType.DMA((3, 8)),
-            pltpu.SemaphoreType.DMA((6,)),
-            pltpu.SemaphoreType.DMA((6,)),
+            pltpu.SemaphoreType.DMA((3,)),
+            pltpu.SemaphoreType.DMA((3,)),
             pltpu.SemaphoreType.DMA((6,)),
             pltpu.SemaphoreType.DMA((6,)),
             pltpu.SemaphoreType.DMA((1,)),

time: 43.5 us -> 42.9 us (0.986)
  Pallas kernels: 40.8 us -> 40.3 us
    pallas_call x1, Pallas kernels: 40.8 us -> 40.3 us  [per_device(): pl.pallas_call(body, out_shape=(pltpu.VMEM((n0, n0, nz), F32), pltpu.VMEM...]
where the time goes in v6:
time: 42.9 us; the launch traced here: 42.8 us
  Pallas kernels  40.3 us (94%)
  local copies, waits for them, and re-layouts  1.87 us (4%)
  between operations  0.64 us (1%)
    pallas_call x1, Pallas kernels, per_device(): pl.pallas_call(body, out_shape=(pltpu.VMEM((n0, n0, nz), F32), pltpu.VMEM...  40.3 us
    unnamed x3, local copies, waits for them, and re-layouts  1.87 us

profile of v6, /device:TPU:1, one launch (start us, length us, event | category | flops | bytes accessed | tf_op | source)
XLA Modules:
  0.0 42.8 jit_solution(9672036040100779089)
XLA Ops:
  0.6 40.3 %vcycle_down.1 = (f32[16,16,128]{2,1,0:T(8,128)S(1)}, f32[8,8,64]{2,1,0:T(8,128)S(1)}, f32[4,4,32]{2,1,0:T(4,128)S(1)}) custom-call(f32[16,16,128]{2,1,0:T(8,128)} %refs_0_.1, f32[16,16,128]{2,1,0:T(8,128)} %refs_1_.1, f32[16,16,128]{2,1,0:T(8,128)} %refs_2_.1, f32[16,16,128]{2,1,0:T(8,128)} %refs_3_.1, f32[16,16,128]{2,1,0:T(8,128)} %refs_4_.1), custom_call_target="tpu_custom_call" | custom-call | flops 40000000 | bytes 800000 | tf_op jit(solution)/shard_map/vcycle_down/pallas_call | solution.py:635
  40.9 0.7 %copy.11 = f32[16,16,128]{2,1,0:T(8,128)} copy(f32[16,16,128]{2,1,0:T(8,128)S(1)} %get-tuple-element.3) | data formatting | bytes 262144
  41.6 0.6 %copy.13 = f32[4,4,32]{2,1,0:T(4,128)} copy(f32[4,4,32]{2,1,0:T(4,128)S(1)} %get-tuple-element.5) | data formatting | bytes 4096
  42.2 0.6 %copy.12 = f32[8,8,64]{2,1,0:T(8,128)} copy(f32[8,8,64]{2,1,0:T(8,128)S(1)} %get-tuple-element.4) | data formatting | bytes 32768

commit v7 on v6

--- a/solution.py
+++ b/solution.py
@@ -440,7 +440,7 @@
     rhs_blocks[1, gy, first4] = mixed
 
     mine = rhs_blocks.at[1, gy, first4]
-    for dx in (1, -1, 0):
+    for dx in (0, 1, -1):
 
         def spread(dx=dx):
             for o in sorted(range(1 if dx == 0 else 0, ny), key=lambda o: -min(o, ny - o)):
@@ -553,7 +553,11 @@
         meanwhile()
         others = slots.at[pl.ds(1, count)]
         bytes_of(others, row_recv.at[k]).wait()
-        return jnp.sum(slots[...], axis=0), bytes_of(others, row_send.at[k])
+        total = slots[...]
+        while total.shape[0] > 1:
+            half = total.shape[0] // 2
+            total = total[:half] + total[half:]
+        return total[0], bytes_of(others, row_send.at[k])
 
     def meanwhile():
         for which, copies in enumerate((sent0, sent1, sent2)):
@@ -570,14 +574,17 @@
     row, sent5 = all_sum(row, gather_x, 0, peer_x)
     moments = [jnp.sum(jnp.where(lane == k, row, 0.0), axis=1, keepdims=True) for k in range(9)]
 
+    def balanced(terms):
+        while len(terms) > 1:
+            pairs = [a + b for a, b in zip(terms[0::2], terms[1::2])]
+            terms = pairs + terms[2 * len(pairs) :]
+        return terms[0]
+
     def inner(u, w):
-        total = None
-        for i, a in enumerate(u):
-            for j, b in enumerate(w):
-                if a is not None and b is not None:
-                    term = a * b * moments[i + j]
-                    total = term if total is None else total + term
-        return total
+        return balanced([
+            a * balanced([b * moments[i + j] for j, b in enumerate(w) if b is not None])
+            for i, a in enumerate(u) if a is not None
+        ])
 
     def plus(u, c, w):
         out = []

time: 42.9 us -> 42.9 us (level)
  no operation moved by 1% of the time
where the time goes in v7:
time: 42.9 us; the launch traced here: 42.8 us
  Pallas kernels  40.2 us (94%)
  local copies, waits for them, and re-layouts  1.87 us (4%)
  between operations  0.64 us (1%)
    pallas_call x1, Pallas kernels, per_device(): pl.pallas_call(body, out_shape=(pltpu.VMEM((n0, n0, nz), F32), pltpu.VMEM...  40.2 us
    unnamed x3, local copies, waits for them, and re-layouts  1.87 us

profile of v7, /device:TPU:1, one launch (start us, length us, event | category | flops | bytes accessed | tf_op | source)
XLA Modules:
  0.0 42.8 jit_solution(5421733614317206435)
XLA Ops:
  0.6 40.2 %vcycle_down.1 = (f32[16,16,128]{2,1,0:T(8,128)S(1)}, f32[8,8,64]{2,1,0:T(8,128)S(1)}, f32[4,4,32]{2,1,0:T(4,128)S(1)}) custom-call(f32[16,16,128]{2,1,0:T(8,128)} %refs_0_.1, f32[16,16,128]{2,1,0:T(8,128)} %refs_1_.1, f32[16,16,128]{2,1,0:T(8,128)} %refs_2_.1, f32[16,16,128]{2,1,0:T(8,128)} %refs_3_.1, f32[16,16,128]{2,1,0:T(8,128)} %refs_4_.1), custom_call_target="tpu_custom_call" | custom-call | flops 40000000 | bytes 800000 | tf_op jit(solution)/shard_map/vcycle_down/pallas_call | solution.py:642
  40.9 0.7 %copy.11 = f32[16,16,128]{2,1,0:T(8,128)} copy(f32[16,16,128]{2,1,0:T(8,128)S(1)} %get-tuple-element.3) | data formatting | bytes 262144
  41.5 0.6 %copy.13 = f32[4,4,32]{2,1,0:T(4,128)} copy(f32[4,4,32]{2,1,0:T(4,128)S(1)} %get-tuple-element.5) | data formatting | bytes 4096
  42.1 0.6 %copy.12 = f32[8,8,64]{2,1,0:T(8,128)} copy(f32[8,8,64]{2,1,0:T(8,128)S(1)} %get-tuple-element.4) | data formatting | bytes 32768

commit v8 on v7

--- a/solution.py
+++ b/solution.py
@@ -535,11 +535,13 @@
         basis[number + 1, here] = coef2[0, here] * x - total
 
     own = pl.ds(HALO, n2)
-    vectors = [basis[i, own, line, :] for i in range(5)]
+    vectors = [basis[i, own] for i in range(5)]
+    col = lax.broadcasted_iota(jnp.int32, basis.shape[2:], 0)
+    inner_cols = jnp.logical_and(col >= HALO, col < HALO + wide)
     lane = lane_of((1, LANES))
     row = jnp.zeros((1, LANES), F32)
     for k in range(9):
-        product = jnp.sum(vectors[k // 2] * vectors[(k + 1) // 2], axis=0)
+        product = jnp.where(inner_cols, jnp.sum(vectors[k // 2] * vectors[(k + 1) // 2], axis=0), 0.0)
         moment = jnp.sum(jnp.sum(product, axis=0, keepdims=True), axis=1, keepdims=True)
         row = jnp.where(lane == k, moment, row)
 
@@ -620,7 +622,7 @@
             term = c * vectors[i]
             total = term if total is None else total + term
     group, place = lax.div(gy, ny // 4), lax.rem(gy, ny // 4)
-    mine = compacted(total, 4, group)
+    mine = compacted(total, 4, group)[:, HALO:]
     bottom = mine[:, :n2]
     for p in range(1, ny // 4):
         bottom = jnp.where(place == p, mine[:, n2 * p : n2 * (p + 1)], bottom)

time: 42.9 us -> 42.9 us (level)
  no operation moved by 1% of the time
where the time goes in v8:
time: 42.9 us; the launch traced here: 42.8 us
  Pallas kernels  40.2 us (94%)
  local copies, waits for them, and re-layouts  1.87 us (4%)
  between operations  0.64 us (1%)
    pallas_call x1, Pallas kernels, per_device(): pl.pallas_call(body, out_shape=(pltpu.VMEM((n0, n0, nz), F32), pltpu.VMEM...  40.2 us
    unnamed x3, local copies, waits for them, and re-layouts  1.87 us

profile of v8, /device:TPU:1, one launch (start us, length us, event | category | flops | bytes accessed | tf_op | source)
XLA Modules:
  0.0 42.8 jit_solution(4362726962645448574)
XLA Ops:
  0.6 40.2 %vcycle_down.1 = (f32[16,16,128]{2,1,0:T(8,128)S(1)}, f32[8,8,64]{2,1,0:T(8,128)S(1)}, f32[4,4,32]{2,1,0:T(4,128)S(1)}) custom-call(f32[16,16,128]{2,1,0:T(8,128)} %refs_0_.1, f32[16,16,128]{2,1,0:T(8,128)} %refs_1_.1, f32[16,16,128]{2,1,0:T(8,128)} %refs_2_.1, f32[16,16,128]{2,1,0:T(8,128)} %refs_3_.1, f32[16,16,128]{2,1,0:T(8,128)} %refs_4_.1), custom_call_target="tpu_custom_call" | custom-call | flops 40000000 | bytes 800000 | tf_op jit(solution)/shard_map/vcycle_down/pallas_call | solution.py:644
  40.9 0.7 %copy.11 = f32[16,16,128]{2,1,0:T(8,128)} copy(f32[16,16,128]{2,1,0:T(8,128)S(1)} %get-tuple-element.3) | data formatting | bytes 262144
  41.5 0.6 %copy.13 = f32[4,4,32]{2,1,0:T(4,128)} copy(f32[4,4,32]{2,1,0:T(4,128)S(1)} %get-tuple-element.5) | data formatting | bytes 4096
  42.1 0.6 %copy.12 = f32[8,8,64]{2,1,0:T(8,128)} copy(f32[8,8,64]{2,1,0:T(8,128)S(1)} %get-tuple-element.4) | data formatting | bytes 32768
